TPU v7x, 512 devices: a whole 4x4x16 slice. The times are simulated.
512 devices in a mesh: crop: 8 (over y, core), row: 16 (over z_lo, x), col: 4 (over z_hi).
Axes of the slice: x: 4, y: 4, z: 16 (z_hi: 4, z_lo: 4; z = z_hi * 4 + z_lo), core: 2. Of those that a mesh axis runs over, the one named last changes fastest.
Arguments:
- pair: bfloat16 [4096, 512, 128], P(('crop', 'row'), 'col'), parts along dimension 0, may hold values from -256 to 256
- norm_gain: float32 [128], replicated, may hold values from 0.5 to 1.5
- norm_bias: float32 [128], replicated, may hold values from -3 to 3
- w_gate: bfloat16 [128, 512], replicated, may hold values from -0.5 to 0.5
- w_up: bfloat16 [128, 512], replicated, may hold values from -0.5 to 0.5
- w_down: bfloat16 [512, 128], replicated, may hold values from -0.25 to 0.25
- head_weight: bfloat16 [1024, 64], P('crop'), parts along dimension 0, may hold values from -1 to 1
- head_bias: float32 [64], replicated, may hold values from -4 to 4
- targets: int32 [4096, 512], P(('crop', 'row'), 'col'), parts along dimension 0, may hold values from 0 to 63
- mask: int32 [4096, 512], P(('crop', 'row'), 'col'), parts along dimension 0, may hold values from 0 to 1
Outputs:
- pair_grad: bfloat16 [4096, 512, 128], P(('crop', 'row'), 'col'), parts along dimension 0
- ln_gain_grad: float32 [1024], P('crop'), parts along dimension 0
- ln_bias_grad: float32 [1024], P('crop'), parts along dimension 0
- w_gate_grad: float32 [1024, 512], P('crop'), parts along dimension 0
- w_up_grad: float32 [1024, 512], P('crop'), parts along dimension 0
- w_down_grad: float32 [4096, 128], P('crop'), parts along dimension 0
- head_weight_grad: float32 [1024, 64], P('crop'), parts along dimension 0
- head_bias_grad: float32 [512], P('crop'), parts along dimension 0
There are 8 independent parts, one for each index of `crop`. A program takes and returns all parts, laid end to end along the dimension named above; an argument that names none is the same for every part. Nothing has to cross between parts.
All inputs are finite; a program needn't handle non-finite values.
Results may differ from a plain program's by a relative error of at most 0.02.
Values may be sent and summed in bfloat16 or wider, within the bound.
No kernel may reach another device: no remote copies, remote signals or barrier semaphores. Data moves between devices by JAX's collectives and lax.ppermute only.
A program may use at most 64 MiB of HBM per device.

v0:
```python
import jax
import jax.numpy as jnp
from jax import lax
from jax.sharding import PartitionSpec as P


def layer_normalize(input_rows, norm_gain, norm_bias):
    input_float = input_rows.astype(jnp.float32)
    centered_input = jnp.mean(input_float, axis=-1, keepdims=True)
    variance = jnp.mean(jnp.square(input_float - centered_input), axis=-1, keepdims=True)
    inverse_deviation = lax.rsqrt(variance + 1e-05)
    standardized_input = (input_float - centered_input) * inverse_deviation
    normalized_rows = (standardized_input * norm_gain + norm_bias).astype(jnp.bfloat16)
    return (input_float, standardized_input, inverse_deviation, normalized_rows)


def mirror_logits(values):
    first = lax.all_to_all(values, "col", split_axis=1, concat_axis=2, tiled=True)
    second = lax.all_to_all(first, ("row", "col"), split_axis=2, concat_axis=1, tiled=True)
    third = lax.all_to_all(second, "col", split_axis=1, concat_axis=2, tiled=True)
    return jnp.swapaxes(third, 1, 2)


def mirror_terms(values):
    first = lax.all_to_all(
        values.astype(jnp.bfloat16), "col", split_axis=1, concat_axis=2, tiled=True
    ).astype(values.dtype)
    second = lax.all_to_all(
        first.astype(jnp.bfloat16), ("row", "col"), split_axis=2, concat_axis=1, tiled=True
    ).astype(first.dtype)
    third = lax.all_to_all(
        second.astype(jnp.bfloat16), "col", split_axis=1, concat_axis=2, tiled=True
    ).astype(second.dtype)
    return jnp.swapaxes(third, 1, 2)


def on_device(
    pair, norm_gain, norm_bias, w_gate, w_up, w_down, head_weight, head_bias, targets, mask
):
    rows_i, cols_j, chans = pair.shape
    bins = head_weight.shape[1]
    hidden_width = w_gate.shape[1]
    pairs = rows_i * cols_j
    block = min(1024, pairs)
    count = pairs // block
    length = rows_i * lax.axis_size("row")
    flat = pair.reshape(count, block, chans)

    def forward_block(input_rows):
        input_float, standardized_input, inverse_deviation, normalized_rows = layer_normalize(
            input_rows, norm_gain, norm_bias
        )
        gate = jnp.dot(normalized_rows, w_gate, preferred_element_type=jnp.float32)
        up = jnp.dot(normalized_rows, w_up, preferred_element_type=jnp.float32)
        hidden = (jax.nn.silu(gate) * up).astype(jnp.bfloat16)
        return (input_float + jnp.dot(hidden, w_down, preferred_element_type=jnp.float32)).astype(
            jnp.bfloat16
        )

    updated = lax.map(forward_block, flat).reshape(pairs, chans)
    half = (
        jnp.einsum("pc,cb->bp", updated, head_weight, preferred_element_type=jnp.float32)
        + head_bias[:, None]
    )
    half = half.astype(jnp.bfloat16).reshape(bins, rows_i, cols_j)
    level = lax.broadcasted_iota(jnp.int32, (bins, 1, 1), 0)
    half_t = mirror_logits(half)
    symmetric = half.astype(jnp.float32) + half_t.astype(jnp.float32)
    prob = jnp.exp(jax.nn.log_softmax(symmetric, axis=0))
    own = mask[None].astype(jnp.float32) * (prob - (level == targets[None]).astype(jnp.float32))
    other = mirror_terms(own)
    half_grad = (own + other).astype(jnp.bfloat16).reshape(bins, pairs)
    head_wsum = jnp.einsum("pc,bp->cb", updated, half_grad, preferred_element_type=jnp.float32)
    head_bsum = jnp.sum(half_grad.astype(jnp.float32), axis=1)
    updated_grad = jnp.einsum(
        "bp,cb->pc", half_grad, head_weight, preferred_element_type=jnp.float32
    )

    def backward_block(carry, inputs):
        gain_accumulated, bias_sum, gate_sum, up_sum, down_sum = carry
        input_rows, grad_in = inputs
        input_float, standardized_input, inverse_deviation, normalized_rows = layer_normalize(
            input_rows, norm_gain, norm_bias
        )
        gate = jnp.dot(normalized_rows, w_gate, preferred_element_type=jnp.float32)
        up = jnp.dot(normalized_rows, w_up, preferred_element_type=jnp.float32)
        silu_gate = jax.nn.silu(gate)
        hidden = (silu_gate * up).astype(jnp.bfloat16)
        grad_b = grad_in.astype(jnp.bfloat16)
        down_sum = down_sum + jnp.einsum(
            "pf,pc->fc", hidden, grad_b, preferred_element_type=jnp.float32
        )
        hidden_grad = jnp.einsum("pc,fc->pf", grad_b, w_down, preferred_element_type=jnp.float32)
        sigma = jax.nn.sigmoid(gate)
        gate_grad = (hidden_grad * up * sigma * (1.0 + gate * (1.0 - sigma))).astype(jnp.bfloat16)
        up_grad = (hidden_grad * silu_gate).astype(jnp.bfloat16)
        gate_sum = gate_sum + jnp.einsum(
            "pc,pf->cf", normalized_rows, gate_grad, preferred_element_type=jnp.float32
        )
        up_sum = up_sum + jnp.einsum(
            "pc,pf->cf", normalized_rows, up_grad, preferred_element_type=jnp.float32
        )
        normalized_gradient = jnp.einsum(
            "pf,cf->pc", gate_grad, w_gate, preferred_element_type=jnp.float32
        ) + jnp.einsum("pf,cf->pc", up_grad, w_up, preferred_element_type=jnp.float32)
        gain_accumulated = gain_accumulated + jnp.sum(
            normalized_gradient * standardized_input, axis=0
        )
        bias_sum = bias_sum + jnp.sum(normalized_gradient, axis=0)
        scaled_rows = normalized_gradient * norm_gain
        backward_pass = inverse_deviation * (
            scaled_rows
            - jnp.mean(scaled_rows, axis=-1, keepdims=True)
            - standardized_input
            * jnp.mean(scaled_rows * standardized_input, axis=-1, keepdims=True)
        )
        result = (grad_in + backward_pass).astype(jnp.bfloat16)
        return ((gain_accumulated, bias_sum, gate_sum, up_sum, down_sum), result)

    start = (
        jnp.zeros((chans,), jnp.float32),
        jnp.zeros((chans,), jnp.float32),
        jnp.zeros((chans, hidden_width), jnp.float32),
        jnp.zeros((chans, hidden_width), jnp.float32),
        jnp.zeros((hidden_width, chans), jnp.float32),
    )
    sums, grads = lax.scan(backward_block, start, (flat, updated_grad.reshape(count, block, chans)))
    pair_grad = grads.reshape(rows_i, cols_j, chans)
    gain_tot, bias_tot, gate_tot, up_tot, down_tot, head_wtot, head_btot = lax.psum(
        (sums[0], sums[1], sums[2], sums[3], sums[4], head_wsum, head_bsum), ("row", "col")
    )
    return (
        pair_grad,
        gain_tot / length,
        bias_tot / length,
        gate_tot / length,
        up_tot / length,
        down_tot / length,
        head_wtot / length,
        head_btot / length,
    )


def solution(mesh):
    in_specs = (
        P(("crop", "row"), "col", None),
        P(),
        P(),
        P(),
        P(),
        P(),
        P("crop", None),
        P(),
        P(("crop", "row"), "col"),
        P(("crop", "row"), "col"),
    )
    out_specs = (
        P(("crop", "row"), "col", None),
        P("crop"),
        P("crop"),
        P("crop", None),
        P("crop", None),
        P("crop", None),
        P("crop", None),
        P("crop"),
    )
    return jax.shard_map(
        on_device, mesh=mesh, in_specs=in_specs, out_specs=out_specs, check_vma=False
    )
```

profile of v0, /device:TPU:32, one launch (start us, length us, event | category | flops | bytes accessed | tf_op | source)
XLA Modules:
  0.0 716.5 jit_solution(2525921857595615485)
XLA Ops:
  7.2 1.1 broadcast.97.clone
  8.3 27.0 %while.31 = (s32[]{:T(128)}, bf16[4,1024,128]{2,1,0:T(8,128)(2,1)}, bf16[4,1024,128]{2,1,0:T(8,128)(2,1)}, f32[128]{0:T(128)}, f32[128]{0:T(128)}, /*index=5*/bf...) while((s32[]{:T(128)}, bf16[4,1024,128]{2,1,0:T(8,128)(2,1)}, ...), condition=%wide.region_3.4_spmd, body=%wide.region_0.3_spmd.sunk | while | flops 408552448 | bytes 10931425 | solution.py:60
  8.3 1.2 convert_reduce_fusion.5
  9.5 1.3 fusion.136
  10.9 1.5 fusion.137
  12.4 2.6 fusion.138
  15.1 1.2 convert_reduce_fusion.5
  16.3 1.3 fusion.136
  17.6 1.5 fusion.137
  19.1 2.6 fusion.138
  21.8 1.2 convert_reduce_fusion.5
  23.0 1.3 fusion.136
  24.3 1.5 fusion.137
  25.9 2.6 fusion.138
  28.6 1.2 convert_reduce_fusion.5
  29.8 1.3 fusion.136
  31.1 1.5 fusion.137
  32.6 2.6 fusion.138
  35.3 1.7 fusion.75
  37.1 46.6 %all_to_all.90 = bf16[64,32,128]{2,0,1:T(8,128)(2,1)S(1)} all-to-all(bf16[64,32,128]{2,0,1:T(8,128)(2,1)S(1)} %bitcast.240), channel_id=1, replica_groups=mesh['crop'=8,'row'=16,'col'=4] {'col'}, dimensions={1} | all-to-all | bytes 1048576 | tf_op jit(solution)/shard_map/all_to_all | solution.py:18
  85.0 40.2 %all_to_all.91 = bf16[64,2,2048]{2,1,0:T(2,128)(2,1)S(1)} all-to-all(bf16[64,2,2048]{2,1,0:T(2,128)(2,1)S(1)} %reshape.98), channel_id=1, replica_groups=mesh['crop'=8,'row'=16,'col'=4] {'row','col'}, dimensions={0} | all-to-all | bytes 1048576 | tf_op jit(solution)/shard_map/all_to_all | solution.py:19
  126.2 1.6 reshape.100
  127.8 3.5 all-to-all-start.2
  131.3 26.2 %all-to-all-done.2 = bf16[4,2,32768]{2,1,0:T(2,128)(2,1)S(1)} async-done(((bf16[4,2,32768]{2,1,0:T(2,128)(2,1)}), bf16[4,2,32768]{2,1,0:T(2,128)(2,1)S(1)}, u32[]{:S(2)}, u32[]{:S(2)}) %all-to-all-start.2) | async-done | bytes 524320 | tf_op jit(solution)/shard_map/all_to_all | solution.py:20
  158.2 1.3 copy.87
  159.6 2.1 fusion.69
  161.7 1.8 fusion.85
  163.5 34.5 %all_to_all.92 = bf16[64,32,128]{2,0,1:T(8,128)(2,1)S(1)} all-to-all(bf16[64,32,128]{2,0,1:T(8,128)(2,1)S(1)} %get-tuple-element.243), channel_id=1, replica_groups=mesh['crop'=8,'row'=16,'col'=4] {'col'}, dimensions={1} | all-to-all | bytes 1048576 | tf_op jit(solution)/shard_map/all_to_all | solution.py:25
  199.3 41.4 %all_to_all.93 = bf16[64,2,2048]{2,1,0:T(2,128)(2,1)S(1)} all-to-all(bf16[64,2,2048]{2,1,0:T(2,128)(2,1)S(1)} %reshape.102), channel_id=1, replica_groups=mesh['crop'=8,'row'=16,'col'=4] {'row','col'}, dimensions={0} | all-to-all | bytes 1048576 | tf_op jit(solution)/shard_map/all_to_all | solution.py:28
  241.6 1.6 reshape.104
  243.2 3.5 all-to-all-start.5
  246.9 28.6 %all-to-all-done.5 = bf16[4,2,32768]{2,1,0:T(2,128)(2,1)S(1)} async-done(((bf16[4,2,32768]{2,1,0:T(2,128)(2,1)}), bf16[4,2,32768]{2,1,0:T(2,128)(2,1)S(1)}, u32[]{:S(2)}, u32[]{:S(2)}) %all-to-all-start.5) | async-done | bytes 524320 | tf_op jit(solution)/shard_map/all_to_all | solution.py:31
  276.3 1.3 copy.92
  279.1 1.1 broadcast.97
  280.3 30.8 %while.32 = (s32[]{:T(128)}, f32[128]{0:T(128)S(1)}, f32[128]{0:T(128)S(1)}, f32[128,512]{1,0:T(8,128)}, f32[128,512]{1,0:T(8,128)}, /*index=5*/f32[512,128]{1,0...) while((s32[]{:T(128)}, f32[128]{0:T(128)S(1)}, ...), condition=%wide.region_13.14_spmd.clone, body=%wide.region_6.13_spmd.clone.sunk | while | flops 1090782464 | bytes 33543568 | solution.py:127
  281.8 0.8 convolution_add_fusion.10
  282.7 1.1 multiply_convert_fusion.8
  286.6 1.3 bitcast_dynamic-update-slice_fusion.2
  290.4 1.1 multiply_convert_fusion.8
  294.3 1.3 bitcast_dynamic-update-slice_fusion.2
  298.1 1.1 multiply_convert_fusion.8
  302.0 1.3 bitcast_dynamic-update-slice_fusion.2
  305.8 1.1 multiply_convert_fusion.8
  309.7 1.3 bitcast_dynamic-update-slice_fusion.2
  311.1 1.7 fusion.83
  312.8 391.7 %all-reduce = (f32[128]{0:T(128)S(1)}, f32[128]{0:T(128)S(1)}, f32[128,64]{0,1:T(8,128)S(1)}, f32[64]{0:T(128)S(1)}) all-reduce(f32[128]{0:T(128)S(1)} %get-tuple-element.129, f32[128]{0:T(128)S(1)} %get-tuple-element.130, f32[128,64]{0,1:T(8,128)S(1)} %fusion.83, ...), channel_id=1, replica_groups=mesh['crop'=8,'row'=16,'col'=4] {'row','col'}, use_global_device_ids=true, to_apply=%region_14.15 | all-reduce | flops 8512 | bytes 68096 | tf_op jit(solution)/shard_map/psum | solution.py:129
  706.1 1.7 broadcast_multiply_fusion.4
  707.8 1.9 broadcast_multiply_fusion.5
  (195 shorter events, 29.2 us)
Async XLA Ops:
  7.2 28.1 %copy-start = (bf16[128,64]{0,1:T(8,128)(2,1)S(1)}, bf16[128,64]{0,1:T(8,128)(2,1)}, u32[]{:S(2)}) copy-start(bf16[128,64]{0,1:T(8,128)(2,1)} %param.20) | copy-start | bytes 49156
  8.3 27.0 %copy-start.19 = (f32[64]{0:T(128)S(1)}, f32[64]{0:T(128)}, u32[]{:S(2)}) copy-start(f32[64]{0:T(128)} %param.21) | copy-start | bytes 772
  8.3 4.1 copy-start.1
  8.3 4.1 copy-start.4
  8.3 4.1 copy-start.11
  8.3 4.1 copy-start.13
  15.0 4.1 copy-start.1
  15.0 4.1 copy-start.4
  15.0 4.1 copy-start.11
  15.0 4.1 copy-start.13
  21.8 4.1 copy-start.1
  21.8 4.1 copy-start.4
  21.8 4.1 copy-start.11
  21.8 4.1 copy-start.13
  28.5 4.1 copy-start.1
  28.5 4.1 copy-start.4
  28.5 4.1 copy-start.11
  28.5 4.1 copy-start.13
  126.0 5.3 copy-start.17
  127.8 29.7 %all-to-all-start.2 = ((bf16[4,2,32768]{2,1,0:T(2,128)(2,1)}), bf16[4,2,32768]{2,1,0:T(2,128)(2,1)S(1)}, u32[]{:S(2)}, u32[]{:S(2)}) async-start(bf16[4,2,32768]{2,1,0:T(2,128)(2,1)} %reshape.100), calls=%async_computation.2 | async-start | bytes 1048576 | tf_op jit(solution)/shard_map/all_to_all | solution.py:20
  159.4 2.2 copy-start.18
  243.2 32.4 %all-to-all-start.5 = ((bf16[4,2,32768]{2,1,0:T(2,128)(2,1)}), bf16[4,2,32768]{2,1,0:T(2,128)(2,1)S(1)}, u32[]{:S(2)}, u32[]{:S(2)}) async-start(bf16[4,2,32768]{2,1,0:T(2,128)(2,1)} %reshape.104), calls=%async_computation.5 | async-start | bytes 1048576 | tf_op jit(solution)/shard_map/all_to_all | solution.py:31
  246.7 459.4 %all-reduce.4.cloned.1.call-start = ((), (), s32[]{:S(2)}) async-start(), calls=%async_computation.6 | async-start | bytes 1572864 | tf_op jit(solution)/shard_map/psum | solution.py:129
  278.5 1.7 copy-start.10
  278.6 1.7 copy-start.2
  278.6 1.7 copy-start.3
  278.6 1.6 copy-start.5
  278.6 1.6 copy-start.12
  278.6 1.6 copy-start.14
  282.7 1.1 copy-start.8
  284.7 1.1 copy-start.9
  284.7 1.1 copy-start.6
  286.6 1.4 copy-start.7
  290.4 1.1 copy-start.16
  290.4 1.2 copy-start.8
  292.3 1.1 copy-start.9
  292.4 1.1 copy-start.6
  294.3 1.4 copy-start.7
  298.1 1.1 copy-start.16
  298.1 1.2 copy-start.8
  300.0 1.1 copy-start.9
  300.0 1.1 copy-start.6
  302.0 1.4 copy-start.7
  305.8 1.1 copy-start.16
  305.8 1.2 copy-start.8
  307.7 1.1 copy-start.9
  307.7 1.1 copy-start.6
  309.7 1.4 copy-start.7
  (9 other events, 8.8 us)
Sparse Core Ops, SparseCore 0:
  311.2 261.3 all-reduce.3
where the time goes:
time: 717 us; the launch traced here: 716 us
  blocking collectives  554 us (77%)
  waiting for transfers between devices  54.8 us (8%)
  matrix products  42.8 us (6%)
  other arithmetic  27.5 us (4%)
  local copies, waits for them, and re-layouts  14.5 us (2%)
  between operations  14.4 us (2%)
    psum x1, blocking collectives, on_device(): lax.psum((sums[0], sums[1], sums[2], sums[3], sums[4], head_wsum, head_bs...  392 us
    all_to_all x1, blocking collectives, mirror_logits(): lax.all_to_all(values, 'col', split_axis=1, concat_axis=2, tiled=True)  46.6 us
    all_to_all x1, blocking collectives, mirror_terms(): lax.all_to_all(first.astype(jnp.bfloat16), ('row', 'col'), split_axis=2,...  41.4 us
    all_to_all x1, blocking collectives, mirror_logits(): lax.all_to_all(first, ('row', 'col'), split_axis=2, concat_axis=1, tiled=...  40.2 us
    all_to_all x1, blocking collectives, mirror_terms(): lax.all_to_all(values.astype(jnp.bfloat16), 'col', split_axis=1, concat_a...  34.5 us
    all_to_all x1, waiting for transfers between devices, mirror_terms(): lax.all_to_all(second.astype(jnp.bfloat16), 'col', split_axis=1, concat_a...  28.6 us
    all_to_all x1, waiting for transfers between devices, mirror_logits(): lax.all_to_all(second, 'col', split_axis=1, concat_axis=2, tiled=True)  26.2 us
  transfers between devices with their start and end apart: 3, of which 2 were waited for; matrix products, arithmetic and copies ran while one was open for 0% of the time, Pallas kernels for 0%

commit v1 on v0

v1 whole, which is shorter than its diff:
```python
import functools

import jax
import jax.numpy as jnp
from jax import lax
from jax.experimental import pallas as pl
from jax.experimental.pallas import tpu as pltpu
from jax.sharding import Mesh, PartitionSpec as P

F32 = jnp.float32
BF16 = jnp.bfloat16
C = 128
FF = 512
NB = 64
SIDE = 32
PAIRS = SIDE * SIDE
SUB = 256
STEPS = PAIRS // SUB
ROWS = SUB // SIDE
WIRE = PAIRS // 2 + 16
GROUP = 16
SHARE = 104
PACK = GROUP * SHARE
GRID_AXES = ("z_lo", "x", "z_hi")
VMEM_LIMIT = 56 * 1024 * 1024


def dot(a, b, a_dim, b_dim):
    return lax.dot_general(
        a, b, (((a_dim,), (b_dim,)), ((), ())), preferred_element_type=F32
    )


def normalize(rows, gain, bias):
    mean = jnp.mean(rows, axis=-1, keepdims=True)
    centered = rows - mean
    variance = jnp.mean(centered * centered, axis=-1, keepdims=True)
    rstd = lax.rsqrt(variance + 1e-05)
    xhat = centered * rstd
    return xhat, rstd, (xhat * gain + bias).astype(BF16)


def sigmoid(v):
    return 0.5 * jnp.tanh(0.5 * v) + 0.5


def spread(ref, start, shift):
    lane = lax.broadcasted_iota(jnp.int32, (8, 128), 1)
    out = jnp.zeros((8, 128), F32)
    for u in range(4):
        rows = ref[pl.ds(start + u, 8, stride=4), :]
        rows = pltpu.roll(rows, lax.rem(shift + 32 * u + 128, 128), 1)
        out = jnp.where((lane >= 32 * u) & (lane < 32 * u + 32), rows, out)
    return out


def send_kernel(
    k_ref, pair_ref, gain_ref, bias_ref, w_gu_ref, w_down_ref, head_ref, head_bias_ref,
    targets_ref, mask_ref, wire_ref, half_ref, codes_ref,
):
    gain, bias = gain_ref[...], bias_ref[...]

    def step(n, _):
        rows = pair_ref[pl.ds(n * ROWS, ROWS)].reshape(SUB, C).astype(F32)
        _, _, normed = normalize(rows, gain, bias)
        gate_up = jnp.dot(normed, w_gu_ref[...], preferred_element_type=F32)
        gate, up = gate_up[:, :FF], gate_up[:, FF:]
        hidden = (gate * sigmoid(gate) * up).astype(BF16)
        updated = (rows + jnp.dot(hidden, w_down_ref[...], preferred_element_type=F32)).astype(BF16)
        half_ref[pl.ds(pl.multiple_of(n * SUB, SUB), SUB), :] = (
            jnp.dot(updated, head_ref[...], preferred_element_type=F32) + head_bias_ref[...]
        )
        return 0

    lax.fori_loop(0, STEPS, step, 0)
    lane = lax.broadcasted_iota(jnp.int32, (SIDE, 128), 1)
    for j in range(SIDE // 2):
        low = half_ref[pl.ds(j, SIDE, stride=SIDE), :]
        high = half_ref[pl.ds(SIDE // 2 + j, SIDE, stride=SIDE), :]
        wire_ref[pl.ds(j * SIDE, SIDE), :] = jnp.where(lane < NB, low, high).astype(BF16)
    codes = jnp.concatenate(
        [targets_ref[...].astype(F32), mask_ref[...].astype(F32), jnp.zeros((64, 128), F32)], axis=0
    )
    codes_ref[...] = codes.T
    start = pl.multiple_of(k_ref[0] * SIDE, SIDE)
    wire_ref[pl.ds(PAIRS // 2, 16), :] = jnp.concatenate(
        [spread(codes_ref, start, 0), spread(codes_ref, start, 96)], axis=0
    ).astype(BF16)


def back_kernel(
    first, last, k_ref, pair_ref, gain_ref, bias_ref, w_gu_ref, w_down_ref, head_ref, head_t_ref,
    head_bias_ref, targets_ref, mask_ref, wire_ref, *rest,
):
    if not first:
        acc_gu_in, acc_down_in, acc_head_in, acc_small_in, _ = rest[:5]
        rest = rest[5:]
    if last:
        pack_ref, grad_ref = rest[:2]
        rest = rest[2:]
    else:
        acc_gu_out, acc_down_out, acc_head_out, acc_small_out, grad_ref = rest[:5]
        rest = rest[5:]
    (normed_s, xhat_s, rstd_s, gate_up_s, hidden_s, updated_s, grad_s, gu_grad_s, codes_s, hg_s, gt_s) = rest
    gain, bias = gain_ref[...], bias_ref[...]

    def forward(n, _):
        at = pl.ds(pl.multiple_of(n * SUB, SUB), SUB)
        rows = pair_ref[pl.ds(n * ROWS, ROWS)].reshape(SUB, C).astype(F32)
        xhat, rstd, normed = normalize(rows, gain, bias)
        normed_s[at, :] = normed
        xhat_s[at, :] = xhat
        rstd_s[at, :] = jnp.broadcast_to(rstd, (SUB, C))
        gate_up = jnp.dot(normed, w_gu_ref[...], preferred_element_type=F32)
        gate_up_s[at, :] = gate_up
        gate, up = gate_up[:, :FF], gate_up[:, FF:]
        hidden = (gate * sigmoid(gate) * up).astype(BF16)
        hidden_s[at, :] = hidden
        updated_s[at, :] = (
            rows + jnp.dot(hidden, w_down_ref[...], preferred_element_type=F32)
        ).astype(BF16)
        return 0

    lax.fori_loop(0, STEPS, forward, 0)

    updated = updated_s[...]
    half = (dot(head_t_ref[...], updated, 1, 1) + head_bias_ref[...]).astype(BF16).astype(F32)
    mirror = wire_ref[pl.ds(0, PAIRS // 2), :].astype(F32).T
    symmetric = half + jnp.concatenate([mirror[:NB], mirror[NB:]], axis=1)
    symmetric = symmetric - jnp.max(symmetric, axis=0, keepdims=True)
    exped = jnp.exp(symmetric)
    prob = exped / jnp.sum(exped, axis=0, keepdims=True)
    shift = lax.rem(128 - k_ref[0] * SIDE, 128)
    codes_s[pl.ds(0, SIDE), :] = targets_ref[...].astype(F32)
    codes_s[pl.ds(SIDE, SIDE), :] = mask_ref[...].astype(F32)
    theirs = wire_ref[pl.ds(PAIRS // 2, 16), :].astype(F32)

    def line(rows):
        return jnp.concatenate([rows[r : r + 1] for r in range(8)], axis=1)

    own_target = line(spread(codes_s, 0, shift))
    own_mask = line(spread(codes_s, SIDE, shift))
    their_target, their_mask = line(theirs[:8]), line(theirs[8:])
    level = lax.broadcasted_iota(jnp.int32, (NB, PAIRS), 0).astype(F32)
    half_grad = (
        own_mask * (prob - jnp.where(level == own_target, 1.0, 0.0))
        + their_mask * (prob - jnp.where(level == their_target, 1.0, 0.0))
    ).astype(BF16)
    hg_s[...] = half_grad
    head_bias_sum = jnp.sum(half_grad.astype(F32), axis=1, keepdims=True)
    grad_s[...] = dot(half_grad, head_t_ref[...], 0, 0)
    grad_t = jnp.dot(head_ref[...], half_grad, preferred_element_type=F32).astype(BF16)
    gt_s[...] = grad_t

    def backward(n, carry):
        gain_sum, bias_sum = carry
        at = pl.ds(pl.multiple_of(n * SUB, SUB), SUB)
        grad_in = grad_s[at, :]
        hidden_grad = dot(grad_in.astype(BF16), w_down_ref[...], 1, 1)
        gate, up = gate_up_s[at, :FF], gate_up_s[at, FF:]
        sigma = sigmoid(gate)
        silu = gate * sigma
        gate_grad = (hidden_grad * up * (sigma * (1.0 + gate * (1.0 - sigma)))).astype(BF16)
        up_grad = (hidden_grad * silu).astype(BF16)
        gu_grad_s[at, :FF] = gate_grad
        gu_grad_s[at, FF:] = up_grad
        normed_grad = dot(gu_grad_s[at, :], w_gu_ref[...], 1, 1)
        xhat, rstd = xhat_s[at, :], rstd_s[at, :]
        product = normed_grad * xhat
        gain_sum = gain_sum + jnp.sum(product, axis=0, keepdims=True)
        bias_sum = bias_sum + jnp.sum(normed_grad, axis=0, keepdims=True)
        scaled = normed_grad * gain
        back = rstd * (
            scaled
            - jnp.mean(scaled, axis=-1, keepdims=True)
            - xhat * jnp.mean(product * gain, axis=-1, keepdims=True)
        )
        grad_ref[pl.ds(n * ROWS, ROWS)] = (grad_in + back).astype(BF16).reshape(ROWS, SIDE, C)
        return gain_sum, bias_sum

    gain_sum, bias_sum = lax.fori_loop(
        0, STEPS, backward, (jnp.zeros((1, C), F32), jnp.zeros((1, C), F32))
    )
    head_sum = jnp.dot(hg_s[...], updated_s[...], preferred_element_type=F32)
    down_sum = jnp.dot(gt_s[...], hidden_s[...], preferred_element_type=F32)
    gu_sum = dot(normed_s[...], gu_grad_s[...], 0, 0)
    head_bias_row = jnp.concatenate(
        [jnp.broadcast_to(head_bias_sum, (NB, 128)), jnp.zeros((NB, 128), F32)], axis=0
    ).T[:1]
    small = jnp.concatenate([gain_sum, bias_sum, head_bias_row, jnp.zeros((5, 128), F32)], axis=0)
    if not first:
        gu_sum = gu_sum + acc_gu_in[...]
        down_sum = down_sum + acc_down_in[...]
        head_sum = head_sum + acc_head_in[...]
        small = small + acc_small_in[...]
    if last:
        for b in range(8):
            pack_ref[pl.ds(b * 128, 128), :] = gu_sum[:, b * 128 : b * 128 + 128].astype(BF16)
        for b in range(4):
            pack_ref[pl.ds(1024 + b * 128, 128), :] = down_sum[:, b * 128 : b * 128 + 128].astype(BF16)
        pack_ref[pl.ds(1536, NB), :] = head_sum.astype(BF16)
        tail = jnp.concatenate([small, jnp.zeros((PACK - 1608, 128), F32)], axis=0)
        pack_ref[pl.ds(1600, PACK - 1600), :] = tail.astype(BF16)
    else:
        acc_gu_out[...] = gu_sum
        acc_down_out[...] = down_sum
        acc_head_out[...] = head_sum
        acc_small_out[...] = small


def unpack_kernel(scale, pack_ref, gain_ref, bias_ref, gate_ref, up_ref, down_ref, head_ref, head_bias_ref):
    def block(b):
        return pack_ref[pl.ds(b * 128, 128), :].astype(F32) * scale

    for b in range(4):
        gate_ref[:, b * 128 : b * 128 + 128] = block(b)
        up_ref[:, b * 128 : b * 128 + 128] = block(4 + b)
        down_ref[pl.ds(b * 128, 128), :] = block(8 + b).T
    tail = block(12)
    head_ref[...] = tail.T[:, :NB]
    gain_ref[...] = tail[NB : NB + 1]
    bias_ref[...] = tail[NB + 1 : NB + 2]
    head_bias_ref[...] = tail[NB + 2 : NB + 3]


def full(shape):
    return pl.BlockSpec(shape, lambda i, k: (0,) * len(shape))


def on_device(
    pair, norm_gain, norm_bias, w_gate, w_up, w_down, head_weight, head_bias, targets, mask
):
    length = SIDE * 16
    place = lax.axis_index("x")
    gain, bias = norm_gain[None], norm_bias[None]
    w_gu = jnp.concatenate([w_gate, w_up], axis=1)
    head_t = head_weight.T
    head_twice = jnp.concatenate([head_weight, head_weight], axis=1)
    head_bias_twice = jnp.concatenate([head_bias, head_bias])[None]
    head_bias_column = head_bias[:, None]
    block = pl.BlockSpec((SIDE, SIDE, C), lambda i, k: (0, k[0], 0))
    params = pltpu.CompilerParams(vmem_limit_bytes=VMEM_LIMIT)

    def send(shift):
        k = lax.rem(place + shift, 4)[None]
        wire = pl.pallas_call(
            send_kernel,
            grid_spec=pltpu.PrefetchScalarGridSpec(
                num_scalar_prefetch=1,
                grid=(1,),
                in_specs=[
                    block, full((1, C)), full((1, C)), full((C, 2 * FF)), full((FF, C)),
                    full((C, 2 * NB)), full((1, 2 * NB)), full((SIDE, 128)), full((SIDE, 128)),
                ],
                out_specs=full((WIRE, 128)),
                scratch_shapes=[pltpu.VMEM((PAIRS, 128), F32), pltpu.VMEM((128, 128), F32)],
            ),
            out_shape=jax.ShapeDtypeStruct((WIRE, 128), BF16),
            compiler_params=params,
            cost_estimate=pl.CostEstimate(
                flops=2 * PAIRS * C * 13 * NB * 2, bytes_accessed=1 << 20, transcendentals=PAIRS * FF
            ),
            name="forward_send",
        )(k, pair, gain, bias, w_gu, w_down, head_twice, head_bias_twice, targets, mask)
        route = [
            ((a * 4 + x) * 4 + b, (b * 4 + (x + shift) % 4) * 4 + a)
            for a in range(4) for x in range(4) for b in range(4)
        ]
        return lax.ppermute(wire, GRID_AXES, route)

    wires = [send(shift) for shift in range(4)]
    sums = [
        jax.ShapeDtypeStruct((C, 2 * FF), F32),
        jax.ShapeDtypeStruct((C, FF), F32),
        jax.ShapeDtypeStruct((NB, C), F32),
        jax.ShapeDtypeStruct((8, C), F32),
    ]
    sum_specs = [full(s.shape) for s in sums]
    state = ()
    for shift in range(4):
        first, last = shift == 0, shift == 3
        k = lax.rem(place + (4 - shift), 4)[None]
        out_shape = [jax.ShapeDtypeStruct((PACK, 128), BF16)] if last else list(sums)
        out_specs = [full((PACK, 128))] if last else list(sum_specs)
        aliases = {}
        if not first:
            aliases[12 + 4] = len(out_shape)
            if not last:
                aliases.update({12 + n: n for n in range(4)})
        state = pl.pallas_call(
            functools.partial(back_kernel, first, last),
            grid_spec=pltpu.PrefetchScalarGridSpec(
                num_scalar_prefetch=1,
                grid=(1,),
                in_specs=[
                    block, full((1, C)), full((1, C)), full((C, 2 * FF)), full((FF, C)),
                    full((C, NB)), full((NB, C)), full((NB, 1)), full((SIDE, 128)), full((SIDE, 128)),
                    full((WIRE, 128)),
                ] + ([] if first else sum_specs + [pl.BlockSpec(memory_space=pl.ANY)]),
                out_specs=out_specs + [block],
                scratch_shapes=[
                    pltpu.VMEM((PAIRS, C), BF16),
                    pltpu.VMEM((PAIRS, C), F32),
                    pltpu.VMEM((PAIRS, C), F32),
                    pltpu.VMEM((PAIRS, 2 * FF), F32),
                    pltpu.VMEM((PAIRS, FF), BF16),
                    pltpu.VMEM((PAIRS, C), BF16),
                    pltpu.VMEM((PAIRS, C), F32),
                    pltpu.VMEM((PAIRS, 2 * FF), BF16),
                    pltpu.VMEM((2 * SIDE, 128), F32),
                    pltpu.VMEM((NB, PAIRS), BF16),
                    pltpu.VMEM((C, PAIRS), BF16),
                ],
            ),
            out_shape=out_shape + [jax.ShapeDtypeStruct(pair.shape, BF16)],
            input_output_aliases=aliases,
            compiler_params=params,
            cost_estimate=pl.CostEstimate(
                flops=2 * PAIRS * C * FF * 11, bytes_accessed=1 << 21, transcendentals=PAIRS * FF
            ),
            name="backward_block",
        )(
            k, pair, gain, bias, w_gu, w_down, head_weight, head_t, head_bias_column, targets, mask,
            wires[shift], *state,
        )
    pack, pair_grad = state

    spread_out = lax.all_to_all(pack.reshape(GROUP, SHARE, 128), ("z_lo", "x"), 0, 0)
    share = jnp.sum(spread_out.astype(F32), axis=0).astype(BF16)
    shares = lax.all_to_all(jnp.broadcast_to(share, (4, SHARE, 128)), "z_hi", 0, 0)
    share = jnp.sum(shares.astype(F32), axis=0).astype(BF16)
    pack = lax.all_to_all(
        jnp.broadcast_to(share, (GROUP, SHARE, 128)), ("z_lo", "x"), 0, 0
    ).reshape(PACK, 128)

    outs = pl.pallas_call(
        functools.partial(unpack_kernel, 1.0 / length),
        out_shape=[
            jax.ShapeDtypeStruct((1, C), F32),
            jax.ShapeDtypeStruct((1, C), F32),
            jax.ShapeDtypeStruct((C, FF), F32),
            jax.ShapeDtypeStruct((C, FF), F32),
            jax.ShapeDtypeStruct((FF, C), F32),
            jax.ShapeDtypeStruct((C, NB), F32),
            jax.ShapeDtypeStruct((1, 128), F32),
        ],
        compiler_params=params,
        name="unpack_sums",
    )(pack)
    gain_tot, bias_tot, gate_tot, up_tot, down_tot, head_tot, head_bias_tot = outs
    return (
        pair_grad, gain_tot[0], bias_tot[0], gate_tot, up_tot, down_tot, head_tot,
        head_bias_tot[0, :NB],
    )


def solution(mesh):
    fine = Mesh(mesh.devices.reshape(8, 4, 4, 4), ("crop",) + GRID_AXES)
    rows = ("crop", "z_lo", "x")
    in_specs = (
        P(rows, "z_hi", None), P(), P(), P(), P(), P(), P("crop", None), P(),
        P(rows, "z_hi"), P(rows, "z_hi"),
    )
    out_specs = (
        P(rows, "z_hi", None), P("crop"), P("crop"), P("crop", None), P("crop", None),
        P("crop", None), P("crop", None), P("crop"),
    )
    return jax.shard_map(
        on_device, mesh=fine, in_specs=in_specs, out_specs=out_specs, check_vma=False
    )
```

time: 717 us -> 158 us (0.22)
  the two profiles are of different devices: /device:TPU:32 before, /device:TPU:8 now
where the time goes in v1:
time: 158 us; the launch traced here: 157 us
  blocking collectives  76.7 us (49%)
  Pallas kernels  57.6 us (36%)
  starting transfers between devices  12.9 us (8%)
  local copies, waits for them, and re-layouts  7.88 us (5%)
    all_to_all x1, blocking collectives, on_device(): lax.all_to_all(pack.reshape(GROUP, SHARE, 128), ('z_lo', 'x'), 0, 0)  36.3 us
    pallas_call x4, Pallas kernels, on_device(): pl.pallas_call(functools.partial(back_kernel, first, last), grid_spec=plt...  34.8 us
    all_to_all x1, blocking collectives, on_device(): lax.all_to_all(jnp.broadcast_to(share, (4, SHARE, 128)), 'z_hi', 0, 0)  25.2 us
    pallas_call x4, Pallas kernels, send(): pl.pallas_call(send_kernel, grid_spec=pltpu.PrefetchScalarGridSpec(num_sc...  20.8 us
    all_to_all x1, blocking collectives, on_device(): lax.all_to_all(jnp.broadcast_to(share, (GROUP, SHARE, 128)), ('z_lo', 'x'...  15.2 us
    ppermute x4, starting transfers between devices, send(): return lax.ppermute(wire, GRID_AXES, route)  12.9 us
    unnamed x23, local copies, waits for them, and re-layouts  6.59 us
  transfers between devices with their start and end apart: 4, of which 0 were waited for; matrix products, arithmetic and copies ran while one was open for 0% of the time, Pallas kernels for 26%

profile of v1, /device:TPU:8, one launch (start us, length us, event | category | flops | bytes accessed | tf_op | source)
XLA Modules:
  0.0 157.3 jit_solution(15269135917894063923)
XLA Ops:
  0.6 0.0 copy-start.3
  0.6 0.0 copy-start.1
  0.7 0.9 constant_dynamic-update-slice_fusion.1
  1.6 0.0 copy-done.3
  1.6 0.1 copy.48.head_ref
  1.7 0.0 copy-start.2
  1.8 0.0 copy-start.4
  1.8 0.7 pad_maximum_fusion.head_ref
  2.5 0.0 copy-done.4
  2.5 0.6 maximum_bitcast_fusion.head_bias_ref
  3.0 0.0 copy-done.2
  3.1 0.0 copy-done.1
  3.1 0.0 copy-start
  3.1 0.7 copy-done
  3.8 5.2 %forward_send.7 = bf16[528,128]{1,0:T(8,128)(2,1)} custom-call(s32[1]{0:T(128)} %bitcast.9.k_ref, bf16[32,128,128]{2,1,0:T(8,128)(2,1)} %pair_ref.15, f32[1,128]{1,0:T(1,128)} %bitcast.23, f32[1,128]{1,0:T(1,128)} %bitcast.31, bf16[128,1024]{1,0:T(8,128)(2,1)} %copy-done, bf16[512,128]{1,0:T(8,128)(2,1)} %w_down_ref.15, ...), custom_call_target="tpu_custom_call" | custom-call | flops 436207616 | bytes 1048576 | tf_op jit(solution)/shard_map/forward_send/pallas_call | solution.py:246
  9.0 1.6 collective-permute-start.3
  10.5 5.2 %forward_send.6 = bf16[528,128]{1,0:T(8,128)(2,1)} custom-call(s32[1]{0:T(128)} %bitcast.k_ref, bf16[32,128,128]{2,1,0:T(8,128)(2,1)} %pair_ref.15, f32[1,128]{1,0:T(1,128)} %bitcast.24, f32[1,128]{1,0:T(1,128)} %bitcast.32, bf16[128,1024]{1,0:T(8,128)(2,1)} %copy-done, bf16[512,128]{1,0:T(8,128)(2,1)} %w_down_ref.15, ...), custom_call_target="tpu_custom_call" | custom-call | flops 436207616 | bytes 1048576 | tf_op jit(solution)/shard_map/forward_send/pallas_call | solution.py:246
  15.7 3.4 %collective-permute-start.2 = (bf16[528,128]{1,0:T(8,128)(2,1)}, bf16[528,128]{1,0:T(8,128)(2,1)S(1)}, u32[]{:S(2)}, u32[]{:S(2)}) collective-permute-start(bf16[528,128]{1,0:T(8,128)(2,1)} %forward_send.6), channel_id=1, source_target_pairs={{0,4},{1,20},{2,36},{3,52},{4,8},{5,24},{6,40},{7,56},{8,12},{9,28... | collective-permute-start | bytes 405512 | tf_op jit(solution)/shard_map/ppermute | solution.py:269
  19.1 5.2 %forward_send.5 = bf16[528,128]{1,0:T(8,128)(2,1)} custom-call(s32[1]{0:T(128)} %bitcast.7.k_ref, bf16[32,128,128]{2,1,0:T(8,128)(2,1)} %pair_ref.15, f32[1,128]{1,0:T(1,128)} %bitcast.25, f32[1,128]{1,0:T(1,128)} %bitcast.33, bf16[128,1024]{1,0:T(8,128)(2,1)} %copy-done, bf16[512,128]{1,0:T(8,128)(2,1)} %w_down_ref.15, ...), custom_call_target="tpu_custom_call" | custom-call | flops 436207616 | bytes 1048576 | tf_op jit(solution)/shard_map/forward_send/pallas_call | solution.py:246
  24.3 4.6 %collective-permute-start.1 = (bf16[528,128]{1,0:T(8,128)(2,1)}, bf16[528,128]{1,0:T(8,128)(2,1)S(1)}, u32[]{:S(2)}, u32[]{:S(2)}) collective-permute-start(bf16[528,128]{1,0:T(8,128)(2,1)} %forward_send.5), channel_id=1, source_target_pairs={{0,8},{1,24},{2,40},{3,56},{4,12},{5,28},{6,44},{7,60},{8,0},{9,16... | collective-permute-start | bytes 405512 | tf_op jit(solution)/shard_map/ppermute | solution.py:269
  28.9 5.2 %forward_send.4 = bf16[528,128]{1,0:T(8,128)(2,1)} custom-call(s32[1]{0:T(128)} %bitcast.5.k_ref, bf16[32,128,128]{2,1,0:T(8,128)(2,1)} %pair_ref.15, f32[1,128]{1,0:T(1,128)} %bitcast.26, f32[1,128]{1,0:T(1,128)} %bitcast.34, bf16[128,1024]{1,0:T(8,128)(2,1)} %copy-done, bf16[512,128]{1,0:T(8,128)(2,1)} %w_down_ref.15, ...), custom_call_target="tpu_custom_call" | custom-call | flops 436207616 | bytes 1048576 | tf_op jit(solution)/shard_map/forward_send/pallas_call | solution.py:246
  34.1 3.3 %collective-permute-start = (bf16[528,128]{1,0:T(8,128)(2,1)}, bf16[528,128]{1,0:T(8,128)(2,1)S(1)}, u32[]{:S(2)}, u32[]{:S(2)}) collective-permute-start(bf16[528,128]{1,0:T(8,128)(2,1)} %forward_send.4), channel_id=1, source_target_pairs={{0,12},{1,28},{2,44},{3,60},{4,0},{5,16},{6,32},{7,48},{8,4},{9,20... | collective-permute-start | bytes 405512 | tf_op jit(solution)/shard_map/ppermute | solution.py:269
  37.5 0.7 copy.49.head_bias_ref
  38.2 0.0 collective-permute-done.3.wire_ref
  38.2 0.0 copy-start.5
  38.2 0.7 copy-done.5
  38.8 8.5 %backward_block.4 = (f32[128,1024]{1,0:T(8,128)}, f32[128,512]{1,0:T(8,128)}, f32[64,128]{1,0:T(8,128)}, f32[8,128]{1,0:T(8,128)}, bf16[32,128,128]{2,1,0:T(8,128)(2,1)}) custom-call(s32[1]{0:T(128)} %bitcast.8.k_ref, bf16[32,128,128]{2,1,0:T(8,128)(2,1)} %pair_ref.15, f32[1,128]{1,0:T(1,128)} %bitcast.27, f32[1,128]{1,0:T(1,128)} %bitcast.35, ...), custom_call_target="tpu_custom_call" | custom-call | flops 1476395008 | bytes 2097152 | tf_op jit(solution)/shard_map/backward_block/pallas_call | solution.py:290
  47.4 0.0 collective-permute-done.2.wire_ref
  47.4 0.0 copy-start.6
  47.4 0.7 copy-done.6
  48.0 8.7 %backward_block.5 = (f32[128,1024]{1,0:T(8,128)}, f32[128,512]{1,0:T(8,128)}, f32[64,128]{1,0:T(8,128)}, f32[8,128]{1,0:T(8,128)}, bf16[32,128,128]{2,1,0:T(8,128)(2,1)}) custom-call(s32[1]{0:T(128)} %bitcast.5.k_ref, bf16[32,128,128]{2,1,0:T(8,128)(2,1)} %pair_ref.15, ...), custom_call_target="tpu_custom_call", output_to_operand_aliasing={{4}: (16, {}), {0}: (12, {}), {1}: (13, {}), {2}: (14, {}),... | custom-call | flops 1476395008 | bytes 2097152 | tf_op jit(solution)/shard_map/backward_block/pallas_call | solution.py:290
  56.8 0.0 collective-permute-done.1.wire_ref
  56.8 0.0 copy-start.7
  56.8 0.6 copy-done.7
  57.5 8.7 %backward_block.6 = (f32[128,1024]{1,0:T(8,128)}, f32[128,512]{1,0:T(8,128)}, f32[64,128]{1,0:T(8,128)}, f32[8,128]{1,0:T(8,128)}, bf16[32,128,128]{2,1,0:T(8,128)(2,1)}) custom-call(s32[1]{0:T(128)} %bitcast.7.k_ref, bf16[32,128,128]{2,1,0:T(8,128)(2,1)} %pair_ref.15, ...), custom_call_target="tpu_custom_call", output_to_operand_aliasing={{4}: (16, {}), {0}: (12, {}), {1}: (13, {}), {2}: (14, {}),... | custom-call | flops 1476395008 | bytes 2097152 | tf_op jit(solution)/shard_map/backward_block/pallas_call | solution.py:290
  66.2 0.0 collective-permute-done.wire_ref
  66.2 0.0 copy-start.8
  66.2 0.6 copy-done.8
  66.9 8.8 %backward_block.7 = (bf16[1664,128]{1,0:T(8,128)(2,1)}, bf16[32,128,128]{2,1,0:T(8,128)(2,1)}) custom-call(s32[1]{0:T(128)} %bitcast.k_ref, bf16[32,128,128]{2,1,0:T(8,128)(2,1)} %pair_ref.15, f32[1,128]{1,0:T(1,128)} %bitcast.30, f32[1,128]{1,0:T(1,128)} %bitcast.38, bf16[128,1024]{1,0:T(8,128)(2,1)} %copy-done, ...), custom_call_target="tpu_custom_call", output_to_operand_aliasing={{1}: (16, {})} | custom-call | flops 1476395008 | bytes 2097152 | tf_op jit(solution)/shard_map/backward_block/pallas_call | solution.py:290
  75.6 36.3 %all_to_all.15 = bf16[16,104,128]{2,1,0:T(8,128)(2,1)S(1)} all-to-all(bf16[16,104,128]{2,1,0:T(8,128)(2,1)} %bitcast.18), channel_id=1, replica_groups=mesh['crop'=8,'z_lo'=4,'x'=4,'z_hi'=4] {'z_lo','x'}, dimensions={0} | all-to-all | bytes 851968 | tf_op jit(solution)/shard_map/all_to_all | solution.py:328
  111.9 0.1 reduce_sum.24
  112.0 25.2 %all_to_all.16 = bf16[4,104,128]{2,1,0:T(8,128)(2,1)S(1)} all-to-all(bf16[4,104,128]{2,1,0:T(8,128)(2,1)S(1)} %broadcast_in_dim.45), channel_id=1, replica_groups=mesh['crop'=8,'z_lo'=4,'x'=4,'z_hi'=4] {'z_hi'}, dimensions={0} | all-to-all | bytes 212992 | tf_op jit(solution)/shard_map/all_to_all | solution.py:330
  137.2 0.1 broadcast_in_dim.46
  137.3 15.2 %all_to_all.17 = bf16[16,104,128]{2,1,0:T(8,128)(2,1)} all-to-all(bf16[16,104,128]{2,1,0:T(8,128)(2,1)S(1)} %broadcast_in_dim.46), channel_id=1, replica_groups=mesh['crop'=8,'z_lo'=4,'x'=4,'z_hi'=4] {'z_lo','x'}, dimensions={0} | all-to-all | bytes 851968 | tf_op jit(solution)/shard_map/all_to_all | solution.py:332
  152.5 2.0 %unpack_sums.1 = (f32[1,128]{1,0:T(1,128)}, f32[1,128]{1,0:T(1,128)}, f32[128,512]{1,0:T(8,128)}, f32[128,512]{1,0:T(8,128)}, f32[512,128]{1,0:T(8,128)}, /*index=5*/f32[128,64]{1,0:T(8,128)}, f32[1,128]{1,0:T(1,128)}) custom-call(bf16[1664,128]{1,0:T(8,128)(2,1)} %bitcast.17), custom_call_target="tpu_custom_call" | custom-call | tf_op jit(solution)/shard_map/unpack_sums/pallas_call | solution.py:336
  154.6 1.5 copy.50
  156.1 0.7 copy-done.9
  156.8 0.5 slice_bitcast_fusion
  (4 shorter events, 0.0 us)
Async XLA Ops:
  0.6 1.0 copy-start.3
  0.6 2.4 %copy-start.1 = (bf16[128,512]{1,0:T(8,128)(2,1)S(1)}, bf16[128,512]{1,0:T(8,128)(2,1)}, u32[]{:S(2)}) copy-start(bf16[128,512]{1,0:T(8,128)(2,1)} %param.14) | copy-start | bytes 393220
  1.7 1.3 copy-start.2
  1.8 0.7 copy-start.4
  3.1 0.7 copy-start
  9.0 29.2 %collective-permute-start.3 = (bf16[528,128]{1,0:T(8,128)(2,1)}, bf16[528,128]{1,0:T(8,128)(2,1)S(1)}, u32[]{:S(2)}, u32[]{:S(2)}) collective-permute-start(bf16[528,128]{1,0:T(8,128)(2,1)} %forward_send.7), channel_id=1, source_target_pairs={{0,0},{1,16},{2,32},{3,48},{4,4},{5,20},{6,36},{7,52},{8,8},{9,24}... | collective-permute-start | bytes 405512 | tf_op jit(solution)/shard_map/ppermute | solution.py:269
  15.7 31.7 %collective-permute-start.2 = (bf16[528,128]{1,0:T(8,128)(2,1)}, bf16[528,128]{1,0:T(8,128)(2,1)S(1)}, u32[]{:S(2)}, u32[]{:S(2)}) collective-permute-start(bf16[528,128]{1,0:T(8,128)(2,1)} %forward_send.6), channel_id=1, source_target_pairs={{0,4},{1,20},{2,36},{3,52},{4,8},{5,24},{6,40},{7,56},{8,12},{9,28... | collective-permute-start | bytes 405512 | tf_op jit(solution)/shard_map/ppermute | solution.py:269
  24.3 32.5 %collective-permute-start.1 = (bf16[528,128]{1,0:T(8,128)(2,1)}, bf16[528,128]{1,0:T(8,128)(2,1)S(1)}, u32[]{:S(2)}, u32[]{:S(2)}) collective-permute-start(bf16[528,128]{1,0:T(8,128)(2,1)} %forward_send.5), channel_id=1, source_target_pairs={{0,8},{1,24},{2,40},{3,56},{4,12},{5,28},{6,44},{7,60},{8,0},{9,16... | collective-permute-start | bytes 405512 | tf_op jit(solution)/shard_map/ppermute | solution.py:269
  34.1 32.1 %collective-permute-start = (bf16[528,128]{1,0:T(8,128)(2,1)}, bf16[528,128]{1,0:T(8,128)(2,1)S(1)}, u32[]{:S(2)}, u32[]{:S(2)}) collective-permute-start(bf16[528,128]{1,0:T(8,128)(2,1)} %forward_send.4), channel_id=1, source_target_pairs={{0,12},{1,28},{2,44},{3,60},{4,0},{5,16},{6,32},{7,48},{8,4},{9,20... | collective-permute-start | bytes 405512 | tf_op jit(solution)/shard_map/ppermute | solution.py:269
  38.2 0.7 copy-start.5
  47.4 0.7 copy-start.6
  56.8 0.7 copy-start.7
  66.2 0.7 copy-start.8
  156.1 0.7 copy-start.9

commit v2 on v1

v2 whole, which is shorter than its diff:
```python
import functools

import jax
import jax.numpy as jnp
from jax import lax
from jax.experimental import pallas as pl
from jax.experimental.pallas import tpu as pltpu
from jax.sharding import Mesh, PartitionSpec as P

F32 = jnp.float32
BF16 = jnp.bfloat16
C = 128
FF = 512
NB = 64
SIDE = 32
PAIRS = SIDE * SIDE
SUB = PAIRS
STEPS = PAIRS // SUB
ROWS = SUB // SIDE
WIRE = PAIRS // 2 + 16
GROUP = 16
SHARE = 104
PACK = GROUP * SHARE
GRID_AXES = ("z_lo", "x", "z_hi")
VMEM_LIMIT = 56 * 1024 * 1024


def dot(a, b, a_dim, b_dim):
    return lax.dot_general(
        a, b, (((a_dim,), (b_dim,)), ((), ())), preferred_element_type=F32
    )


def normalize(rows, gain, bias):
    mean = jnp.mean(rows, axis=-1, keepdims=True)
    centered = rows - mean
    variance = jnp.mean(centered * centered, axis=-1, keepdims=True)
    rstd = lax.rsqrt(variance + 1e-05)
    xhat = centered * rstd
    return xhat, rstd, (xhat * gain + bias).astype(BF16)


def sigmoid(v):
    return 0.5 * jnp.tanh(0.5 * v) + 0.5


def spread(ref, start, shift):
    lane = lax.broadcasted_iota(jnp.int32, (8, 128), 1)
    out = jnp.zeros((8, 128), F32)
    for u in range(4):
        rows = ref[pl.ds(start + u, 8, stride=4), :]
        rows = pltpu.roll(rows, lax.rem(shift + 32 * u + 128, 128), 1)
        out = jnp.where((lane >= 32 * u) & (lane < 32 * u + 32), rows, out)
    return out


def send_kernel(
    k_ref, pair_ref, gain_ref, bias_ref, w_gate_ref, w_up_ref, w_down_ref, head_t_ref, head_bias_ref,
    targets_ref, mask_ref, *rest,
):
    wire_refs, (w_gu_ref, half_ref, codes_ref) = rest[:2], rest[2:]
    turn = pl.program_id(0)

    @pl.when(turn == 0)
    def _():
        w_gu_ref[:, :FF] = w_gate_ref[...]
        w_gu_ref[:, FF:] = w_up_ref[...]
        codes = jnp.concatenate(
            [targets_ref[...].astype(F32), mask_ref[...].astype(F32), jnp.zeros((64, 128), F32)],
            axis=0,
        )
        codes_ref[...] = codes.T

    head_twice = jnp.concatenate([head_t_ref[...], head_t_ref[...]], axis=0)
    head_bias = jnp.concatenate([head_bias_ref[...], head_bias_ref[...]], axis=1)
    rows = pair_ref[...].reshape(PAIRS, C).astype(F32)
    _, _, normed = normalize(rows, gain_ref[...], bias_ref[...])
    gate_up = jnp.dot(normed, w_gu_ref[...], preferred_element_type=F32)
    gate, up = gate_up[:, :FF], gate_up[:, FF:]
    hidden = (gate * sigmoid(gate) * up).astype(BF16)
    updated = (rows + jnp.dot(hidden, w_down_ref[...], preferred_element_type=F32)).astype(BF16)
    half_ref[...] = dot(updated, head_twice, 1, 1) + head_bias
    lane = lax.broadcasted_iota(jnp.int32, (SIDE, 128), 1)
    start = pl.multiple_of(k_ref[turn] * SIDE, SIDE)

    def write(wire_ref):
        for j in range(SIDE // 2):
            low = half_ref[pl.ds(j, SIDE, stride=SIDE), :]
            high = half_ref[pl.ds(SIDE // 2 + j, SIDE, stride=SIDE), :]
            wire_ref[pl.ds(j * SIDE, SIDE), :] = jnp.where(lane < NB, low, high).astype(BF16)
        wire_ref[pl.ds(PAIRS // 2, 16), :] = jnp.concatenate(
            [spread(codes_ref, start, 0), spread(codes_ref, start, 96)], axis=0
        ).astype(BF16)

    for n in range(2):
        pl.when(turn == n)(functools.partial(write, wire_refs[n]))


def back_kernel(
    first, k_ref, pair_ref, gain_ref, bias_ref, w_gate_ref, w_up_ref, w_down_ref, head_t_ref,
    head_bias_ref, targets_ref, mask_ref, wire_a_ref, wire_b_ref, *rest,
):
    turn = pl.program_id(0)
    if first:
        *acc_outs, grad_ref = rest[:5]
        rest = rest[5:]
    else:
        *acc_ins, _, pack_ref, grad_ref = rest[:7]
        rest = rest[7:]
    (acc_gu, acc_down, acc_head, acc_small, w_gu_ref, normed_s, xhat_s, rstd_s, gate_up_s, hidden_s,
     updated_s, grad_s, gu_grad_s, codes_s, half_grad_s, grad_t_s) = rest
    accs = (acc_gu, acc_down, acc_head, acc_small)

    @pl.when(turn == 0)
    def _():
        w_gu_ref[:, :FF] = w_gate_ref[...]
        w_gu_ref[:, FF:] = w_up_ref[...]
        for n, acc in enumerate(accs):
            acc[...] = jnp.zeros(acc.shape, F32) if first else acc_ins[n][...]

    gain, bias = gain_ref[...], bias_ref[...]
    head_bias = jnp.concatenate([head_bias_ref[...], head_bias_ref[...]], axis=1)
    head_bias = jnp.broadcast_to(head_bias, (128, 128)).T[:NB, :1]

    def forward(n, _):
        at = pl.ds(pl.multiple_of(n * SUB, SUB), SUB)
        rows = pair_ref[pl.ds(n * ROWS, ROWS)].reshape(SUB, C).astype(F32)
        xhat, rstd, normed = normalize(rows, gain, bias)
        normed_s[at, :] = normed
        xhat_s[at, :] = xhat
        rstd_s[at, :] = jnp.broadcast_to(rstd, (SUB, C))
        gate_up = jnp.dot(normed, w_gu_ref[...], preferred_element_type=F32)
        gate_up_s[at, :] = gate_up
        gate, up = gate_up[:, :FF], gate_up[:, FF:]
        hidden = (gate * sigmoid(gate) * up).astype(BF16)
        hidden_s[at, :] = hidden
        updated_s[at, :] = (
            rows + jnp.dot(hidden, w_down_ref[...], preferred_element_type=F32)
        ).astype(BF16)
        return 0

    lax.fori_loop(0, STEPS, forward, 0)

    updated = updated_s[...]
    half = (dot(head_t_ref[...], updated, 1, 1) + head_bias).astype(BF16).astype(F32)
    wire = jnp.where(turn == 0, wire_a_ref[...].astype(F32), wire_b_ref[...].astype(F32))
    mirror = wire[: PAIRS // 2].T
    symmetric = half + jnp.concatenate([mirror[:NB], mirror[NB:]], axis=1)
    symmetric = symmetric - jnp.max(symmetric, axis=0, keepdims=True)
    exped = jnp.exp(symmetric)
    prob = exped / jnp.sum(exped, axis=0, keepdims=True)
    shift = lax.rem(128 - k_ref[turn] * SIDE, 128)
    codes_s[pl.ds(0, SIDE), :] = targets_ref[...].astype(F32)
    codes_s[pl.ds(SIDE, SIDE), :] = mask_ref[...].astype(F32)
    theirs = wire[PAIRS // 2 :]

    def line(rows):
        return jnp.concatenate([rows[r : r + 1] for r in range(8)], axis=1)

    own_target = line(spread(codes_s, 0, shift))
    own_mask = line(spread(codes_s, SIDE, shift))
    their_target, their_mask = line(theirs[:8]), line(theirs[8:])
    level = lax.broadcasted_iota(jnp.int32, (NB, PAIRS), 0).astype(F32)
    half_grad = (
        own_mask * (prob - jnp.where(level == own_target, 1.0, 0.0))
        + their_mask * (prob - jnp.where(level == their_target, 1.0, 0.0))
    ).astype(BF16)
    half_grad_s[...] = half_grad
    head_bias_sum = jnp.sum(half_grad.astype(F32), axis=1, keepdims=True)
    grad_s[...] = dot(half_grad, head_t_ref[...], 0, 0)
    grad_t = dot(head_t_ref[...], half_grad, 0, 0).astype(BF16)
    grad_t_s[...] = grad_t

    def backward(n, carry):
        gain_sum, bias_sum = carry
        at = pl.ds(pl.multiple_of(n * SUB, SUB), SUB)
        grad_in = grad_s[at, :]
        hidden_grad = dot(grad_in.astype(BF16), w_down_ref[...], 1, 1)
        gate, up = gate_up_s[at, :FF], gate_up_s[at, FF:]
        sigma = sigmoid(gate)
        silu = gate * sigma
        gate_grad = (hidden_grad * up * (sigma * (1.0 + gate * (1.0 - sigma)))).astype(BF16)
        up_grad = (hidden_grad * silu).astype(BF16)
        gu_grad_s[at, :FF] = gate_grad
        gu_grad_s[at, FF:] = up_grad
        normed_grad = dot(gu_grad_s[at, :], w_gu_ref[...], 1, 1)
        xhat, rstd = xhat_s[at, :], rstd_s[at, :]
        product = normed_grad * xhat
        gain_sum = gain_sum + jnp.sum(product, axis=0, keepdims=True)
        bias_sum = bias_sum + jnp.sum(normed_grad, axis=0, keepdims=True)
        scaled = normed_grad * gain
        back = rstd * (
            scaled
            - jnp.mean(scaled, axis=-1, keepdims=True)
            - xhat * jnp.mean(product * gain, axis=-1, keepdims=True)
        )
        grad_ref[pl.ds(n * ROWS, ROWS)] = (grad_in + back).astype(BF16).reshape(ROWS, SIDE, C)
        return gain_sum, bias_sum

    gain_sum, bias_sum = lax.fori_loop(
        0, STEPS, backward, (jnp.zeros((1, C), F32), jnp.zeros((1, C), F32))
    )
    head_sum = jnp.dot(half_grad_s[...], updated_s[...], preferred_element_type=F32)
    down_sum = jnp.dot(grad_t_s[...], hidden_s[...], preferred_element_type=F32)
    gu_sum = dot(normed_s[...], gu_grad_s[...], 0, 0)
    head_bias_row = jnp.concatenate(
        [jnp.broadcast_to(head_bias_sum, (NB, 128)), jnp.zeros((NB, 128), F32)], axis=0
    ).T[:1]
    small = jnp.concatenate([gain_sum, bias_sum, head_bias_row, jnp.zeros((5, 128), F32)], axis=0)
    acc_gu[...] += gu_sum
    acc_down[...] += down_sum
    acc_head[...] += head_sum
    acc_small[...] += small

    @pl.when(turn == 1)
    def _():
        if first:
            for acc, out in zip(accs, acc_outs):
                out[...] = acc[...]
        else:
            for b in range(8):
                pack_ref[pl.ds(b * 128, 128), :] = acc_gu[:, b * 128 : b * 128 + 128].astype(BF16)
            for b in range(4):
                pack_ref[pl.ds(1024 + b * 128, 128), :] = acc_down[
                    :, b * 128 : b * 128 + 128
                ].astype(BF16)
            pack_ref[pl.ds(1536, NB), :] = acc_head[...].astype(BF16)
            tail = jnp.concatenate([acc_small[...], jnp.zeros((PACK - 1608, 128), F32)], axis=0)
            pack_ref[pl.ds(1600, PACK - 1600), :] = tail.astype(BF16)


def unpack_kernel(scale, pack_ref, gain_ref, bias_ref, gate_ref, up_ref, down_ref, head_ref, head_bias_ref):
    def block(b):
        return pack_ref[pl.ds(b * 128, 128), :].astype(F32) * scale

    for b in range(4):
        gate_ref[:, b * 128 : b * 128 + 128] = block(b)
        up_ref[:, b * 128 : b * 128 + 128] = block(4 + b)
        down_ref[pl.ds(b * 128, 128), :] = block(8 + b).T
    tail = block(12)
    head_ref[...] = tail[:NB]
    gain_ref[...] = tail[NB : NB + 1]
    bias_ref[...] = tail[NB + 1 : NB + 2]
    head_bias_ref[...] = tail[NB + 2 : NB + 3, :NB]


def full(shape):
    return pl.BlockSpec(shape, lambda i, k: (0,) * len(shape))


def on_device(
    pair, norm_gain, norm_bias, w_gate, w_up, w_down, head_weight, head_bias, targets, mask
):
    length = SIDE * 16
    place = lax.axis_index("x")
    params = pltpu.CompilerParams(vmem_limit_bytes=VMEM_LIMIT)
    common = (
        pair, norm_gain[None], norm_bias[None], w_gate, w_up, w_down, head_weight.T, head_bias[None],
        targets, mask,
    )
    block = pl.BlockSpec((SIDE, SIDE, C), lambda i, k: (0, k[i], 0))
    common_specs = [block] + [full(a.shape) for a in common[1:]]

    def send(shift, blocks):
        wires = pl.pallas_call(
            send_kernel,
            grid_spec=pltpu.PrefetchScalarGridSpec(
                num_scalar_prefetch=1,
                grid=(2,),
                in_specs=common_specs,
                out_specs=[full((WIRE, 128))] * 2,
                scratch_shapes=[
                    pltpu.VMEM((C, 2 * FF), BF16),
                    pltpu.VMEM((PAIRS, 128), F32),
                    pltpu.VMEM((128, 128), F32),
                ],
            ),
            out_shape=[jax.ShapeDtypeStruct((WIRE, 128), BF16)] * 2,
            compiler_params=params,
            name="forward_send",
        )(blocks, *common)
        routes = [
            [
                ((a * 4 + x) * 4 + b, (b * 4 + (x + shift + n) % 4) * 4 + a)
                for a in range(4) for x in range(4) for b in range(4)
            ]
            for n in range(2)
        ]
        return wires, [lax.ppermute(wire, GRID_AXES, route) for wire, route in zip(wires, routes)]

    near = lax.rem(place + jnp.arange(4, dtype=jnp.int32), 4)
    early, wires = send(0, near[:2])
    later, _ = lax.optimization_barrier((near[2:], early))
    wires = wires + send(2, later)[1]
    sums = [
        jax.ShapeDtypeStruct((C, 2 * FF), F32),
        jax.ShapeDtypeStruct((C, FF), F32),
        jax.ShapeDtypeStruct((NB, C), F32),
        jax.ShapeDtypeStruct((8, C), F32),
    ]
    sum_specs = [full(a.shape) for a in sums]
    state = ()
    for first in (True, False):
        shift = 0 if first else 2
        out_shape = sums if first else [jax.ShapeDtypeStruct((PACK, 128), BF16)]
        out_specs = [full(a.shape) for a in out_shape]
        state = pl.pallas_call(
            functools.partial(back_kernel, first),
            grid_spec=pltpu.PrefetchScalarGridSpec(
                num_scalar_prefetch=1,
                grid=(2,),
                in_specs=common_specs
                + [full((WIRE, 128))] * 2
                + ([] if first else sum_specs + [pl.BlockSpec(memory_space=pl.ANY)]),
                out_specs=out_specs + [block],
                scratch_shapes=[pltpu.VMEM(a.shape, F32) for a in sums]
                + [
                    pltpu.VMEM((C, 2 * FF), BF16),
                    pltpu.VMEM((PAIRS, C), BF16),
                    pltpu.VMEM((PAIRS, C), F32),
                    pltpu.VMEM((PAIRS, C), F32),
                    pltpu.VMEM((PAIRS, 2 * FF), F32),
                    pltpu.VMEM((PAIRS, FF), BF16),
                    pltpu.VMEM((PAIRS, C), BF16),
                    pltpu.VMEM((PAIRS, C), F32),
                    pltpu.VMEM((PAIRS, 2 * FF), BF16),
                    pltpu.VMEM((2 * SIDE, 128), F32),
                    pltpu.VMEM((NB, PAIRS), BF16),
                    pltpu.VMEM((C, PAIRS), BF16),
                ],
            ),
            out_shape=out_shape + [jax.ShapeDtypeStruct(pair.shape, BF16)],
            input_output_aliases={} if first else {17: 1},
            compiler_params=params,
            name="backward_blocks",
        )(
            lax.rem(place + 4 - shift - jnp.arange(2, dtype=jnp.int32), 4), *common,
            wires[shift], wires[shift + 1], *state,
        )
    pack, pair_grad = state

    spread_out = lax.all_to_all(pack.reshape(GROUP, SHARE, 128), ("z_lo", "x"), 0, 0)
    share = jnp.sum(spread_out.astype(F32), axis=0).astype(BF16)
    shares = lax.all_gather(share, "z_hi")
    share = jnp.sum(shares.astype(F32), axis=0).astype(BF16)
    pack = lax.all_to_all(
        jnp.broadcast_to(share, (GROUP, SHARE, 128)), ("z_lo", "x"), 0, 0
    ).reshape(PACK, 128)

    outs = pl.pallas_call(
        functools.partial(unpack_kernel, 1.0 / length),
        out_shape=[
            jax.ShapeDtypeStruct((1, C), F32),
            jax.ShapeDtypeStruct((1, C), F32),
            jax.ShapeDtypeStruct((C, FF), F32),
            jax.ShapeDtypeStruct((C, FF), F32),
            jax.ShapeDtypeStruct((FF, C), F32),
            jax.ShapeDtypeStruct((NB, C), F32),
            jax.ShapeDtypeStruct((1, NB), F32),
        ],
        compiler_params=params,
        name="unpack_sums",
    )(pack)
    gain_tot, bias_tot, gate_tot, up_tot, down_tot, head_tot, head_bias_tot = outs
    return (
        pair_grad, gain_tot[0], bias_tot[0], gate_tot, up_tot, down_tot, head_tot.T,
        head_bias_tot[0],
    )


def solution(mesh):
    fine = Mesh(mesh.devices.reshape(8, 4, 4, 4), ("crop",) + GRID_AXES)
    rows = ("crop", "z_lo", "x")
    in_specs = (
        P(rows, "z_hi", None), P(), P(), P(), P(), P(), P("crop", None), P(),
        P(rows, "z_hi"), P(rows, "z_hi"),
    )
    out_specs = (
        P(rows, "z_hi", None), P("crop"), P("crop"), P("crop", None), P("crop", None),
        P("crop", None), P("crop", None), P("crop"),
    )
    return jax.shard_map(
        on_device, mesh=fine, in_specs=in_specs, out_specs=out_specs, check_vma=False
    )
```

time: 158 us -> 132 us (0.84)
  Pallas kernels: 57.6 us -> 35.9 us
  local copies, waits for them, and re-layouts: 7.88 us -> 2.61 us
  blocking collectives: 76.7 us -> 78.4 us
    all_to_all x1 -> x0, blocking collectives: 25.2 us -> none  [on_device(): lax.all_to_all(jnp.broadcast_to(share, (4, SHARE, 128)), 'z_hi', 0, 0)]
    all_gather x0 -> x1, blocking collectives: none -> 17.6 us  [on_device(): shares = lax.all_gather(share, 'z_hi')]
    pallas_call x4 -> x2, Pallas kernels: 34.8 us -> 20.9 us  [on_device(): pl.pallas_call(functools.partial(back_kernel, first), grid_spec=pltpu.Pre...]
    all_to_all x1, blocking collectives: 36.3 us -> 45.3 us  [on_device(): lax.all_to_all(pack.reshape(GROUP, SHARE, 128), ('z_lo', 'x'), 0, 0)]
    pallas_call x4 -> x2, Pallas kernels: 20.8 us -> 13 us  [send(): pl.pallas_call(send_kernel, grid_spec=pltpu.PrefetchScalarGridSpec(num_sc...]
    unnamed x23 -> x8, local copies, waits for them, and re-layouts: 6.59 us -> 1.97 us
  transfers between devices with their start and end apart: 4 -> 4, of which waited for: 0 -> 0; matrix products, arithmetic and copies ran while one was open for 0% -> 1% of each run, Pallas kernels for 26% -> 13%
where the time goes in v2:
time: 132 us
  blocking collectives  78.4 us (59%)
  Pallas kernels  35.9 us (27%)
  starting transfers between devices  12.9 us (10%)
  local copies, waits for them, and re-layouts  2.61 us (2%)
    all_to_all x1, blocking collectives, on_device(): lax.all_to_all(pack.reshape(GROUP, SHARE, 128), ('z_lo', 'x'), 0, 0)  45.3 us
    pallas_call x2, Pallas kernels, on_device(): pl.pallas_call(functools.partial(back_kernel, first), grid_spec=pltpu.Pre...  20.9 us
    all_gather x1, blocking collectives, on_device(): shares = lax.all_gather(share, 'z_hi')  17.6 us
    all_to_all x1, blocking collectives, on_device(): lax.all_to_all(jnp.broadcast_to(share, (GROUP, SHARE, 128)), ('z_lo', 'x'...  15.5 us
    pallas_call x2, Pallas kernels, send(): pl.pallas_call(send_kernel, grid_spec=pltpu.PrefetchScalarGridSpec(num_sc...  13 us
    ppermute x4, starting transfers between devices, send(): lax.ppermute(wire, GRID_AXES, route)  12.9 us
  transfers between devices with their start and end apart: 4, of which 0 were waited for; matrix products, arithmetic and copies ran while one was open for 1% of the time, Pallas kernels for 13%

profile of v2, /device:TPU:8, one launch (start us, length us, event | category | flops | bytes accessed | tf_op | source)
XLA Modules:
  0.0 131.7 jit_solution(16866114467949156539)
XLA Ops:
  0.7 0.6 fusion.3
  1.2 6.5 %forward_send.2 = (bf16[528,128]{1,0:T(8,128)(2,1)}, bf16[528,128]{1,0:T(8,128)(2,1)}) custom-call(s32[2]{0:T(128)} %get-tuple-element.46.k_ref, bf16[32,128,128]{2,1,0:T(8,128)(2,1)} %pair_ref.7, f32[1,128]{1,0:T(1,128)} %bitcast.18, f32[1,128]{1,0:T(1,128)} %bitcast.22, bf16[128,512]{1,0:T(8,128)(2,1)} %w_gate_ref.7, bf16[128,512]{1,0:T(8,128)(2,1)} %w_up_ref.7, ...), custom_call_target="tpu_custom_call" | custom-call | tf_op jit(solution)/shard_map/forward_send/pallas_call | solution.py:265
  7.7 1.6 %collective-permute-start.2 = (bf16[528,128]{1,0:T(8,128)(2,1)}, bf16[528,128]{1,0:T(8,128)(2,1)S(1)}, u32[]{:S(2)}, u32[]{:S(2)}) collective-permute-start(bf16[528,128]{1,0:T(8,128)(2,1)} %get-tuple-element.27), channel_id=1, source_target_pairs={{0,0},{1,16},{2,32},{3,48},{4,4},{5,20},{6,36},{7,52},{8,8},{9,24}... | collective-permute-start | bytes 405512 | tf_op jit(solution)/shard_map/ppermute | solution.py:289
  9.3 3.4 %collective-permute-start.3 = (bf16[528,128]{1,0:T(8,128)(2,1)}, bf16[528,128]{1,0:T(8,128)(2,1)S(1)}, u32[]{:S(2)}, u32[]{:S(2)}) collective-permute-start(bf16[528,128]{1,0:T(8,128)(2,1)} %get-tuple-element.28), channel_id=1, source_target_pairs={{0,4},{1,20},{2,36},{3,52},{4,8},{5,24},{6,40},{7,56},{8,12},{9,28... | collective-permute-start | bytes 405512 | tf_op jit(solution)/shard_map/ppermute | solution.py:289
  12.7 6.5 %forward_send.3 = (bf16[528,128]{1,0:T(8,128)(2,1)}, bf16[528,128]{1,0:T(8,128)(2,1)}) custom-call(s32[2]{0:T(128)} %get-tuple-element.29.k_ref, bf16[32,128,128]{2,1,0:T(8,128)(2,1)} %pair_ref.7, f32[1,128]{1,0:T(1,128)} %bitcast.19, f32[1,128]{1,0:T(1,128)} %bitcast.23, bf16[128,512]{1,0:T(8,128)(2,1)} %w_gate_ref.7, bf16[128,512]{1,0:T(8,128)(2,1)} %w_up_ref.7, ...), custom_call_target="tpu_custom_call" | custom-call | tf_op jit(solution)/shard_map/forward_send/pallas_call | solution.py:265
  19.2 4.6 %collective-permute-start = (bf16[528,128]{1,0:T(8,128)(2,1)}, bf16[528,128]{1,0:T(8,128)(2,1)S(1)}, u32[]{:S(2)}, u32[]{:S(2)}) collective-permute-start(bf16[528,128]{1,0:T(8,128)(2,1)} %get-tuple-element.30), channel_id=1, source_target_pairs={{0,8},{1,24},{2,40},{3,56},{4,12},{5,28},{6,44},{7,60},{8,0},{9,16... | collective-permute-start | bytes 405512 | tf_op jit(solution)/shard_map/ppermute | solution.py:289
  23.8 3.3 %collective-permute-start.1 = (bf16[528,128]{1,0:T(8,128)(2,1)}, bf16[528,128]{1,0:T(8,128)(2,1)S(1)}, u32[]{:S(2)}, u32[]{:S(2)}) collective-permute-start(bf16[528,128]{1,0:T(8,128)(2,1)} %get-tuple-element.31), channel_id=1, source_target_pairs={{0,12},{1,28},{2,44},{3,60},{4,0},{5,16},{6,32},{7,48},{8,4},{9,20... | collective-permute-start | bytes 405512 | tf_op jit(solution)/shard_map/ppermute | solution.py:289
  27.2 0.5 compare_select_fusion.4.k_ref
  27.7 0.5 compare_select_fusion.k_ref
  28.2 0.0 collective-permute-done.2.wire_a_ref
  28.2 0.0 copy-start
  28.2 0.0 collective-permute-done.3.wire_b_ref
  28.2 0.6 copy-done
  28.9 0.0 copy-start.1
  28.9 0.6 copy-done.1
  29.5 10.4 %backward_blocks.2 = (f32[128,1024]{1,0:T(8,128)}, f32[128,512]{1,0:T(8,128)}, f32[64,128]{1,0:T(8,128)}, f32[8,128]{1,0:T(8,128)}, bf16[32,128,128]{2,1,0:T(8,128)(2,1)}) custom-call(s32[2]{0:T(128)} %compare_select_fusion.k_ref, bf16[32,128,128]{2,1,0:T(8,128)(2,1)} %pair_ref.7, f32[1,128]{1,0:T(1,128)} %bitcast.20, f32[1,128]{1,0:T(1,128)} %bitcast.24, ...), custom_call_target="tpu_custom_call" | custom-call | tf_op jit(solution)/shard_map/backward_blocks/pallas_call | solution.py:307
  39.9 0.0 collective-permute-done.wire_a_ref
  39.9 0.0 copy-start.2
  39.9 0.0 collective-permute-done.1.wire_b_ref
  40.0 0.0 copy-start.3
  40.0 0.6 copy-done.2
  40.6 0.0 copy-done.3
  40.6 10.5 %backward_blocks.3 = (bf16[1664,128]{1,0:T(8,128)(2,1)}, bf16[32,128,128]{2,1,0:T(8,128)(2,1)}) custom-call(s32[2]{0:T(128)} %compare_select_fusion.4.k_ref, bf16[32,128,128]{2,1,0:T(8,128)(2,1)} %pair_ref.7, f32[1,128]{1,0:T(1,128)} %bitcast.21, f32[1,128]{1,0:T(1,128)} %bitcast.25, bf16[128,512]{1,0:T(8,128)(2,1)} %w_gate_ref.7, ...), custom_call_target="tpu_custom_call", output_to_operand_aliasing={{1}: (17, {})} | custom-call | tf_op jit(solution)/shard_map/backward_blocks/pallas_call | solution.py:307
  51.2 45.3 %all_to_all.10 = bf16[16,104,128]{2,1,0:T(8,128)(2,1)S(1)} all-to-all(bf16[16,104,128]{2,1,0:T(8,128)(2,1)} %bitcast.13), channel_id=1, replica_groups=mesh['crop'=8,'z_lo'=4,'x'=4,'z_hi'=4] {'z_lo','x'}, dimensions={0} | all-to-all | bytes 851968 | tf_op jit(solution)/shard_map/all_to_all | solution.py:342
  96.4 0.1 reduce_sum.24
  96.5 17.6 %all-gather = bf16[416,128]{1,0:T(8,128)(2,1)S(1)} all-gather(bf16[104,128]{1,0:T(8,128)(2,1)S(1)} %reduce_sum.24), channel_id=2, replica_groups=mesh['crop'=8,'z_lo'=4,'x'=4,'z_hi'=4] {'z_hi'}, dimensions={0}, use_global_device_ids=true | all-gather | bytes 133120 | tf_op jit(solution)/shard_map/all_gather | solution.py:344
  114.1 0.1 broadcast_in_dim.15
  114.2 15.5 %all_to_all.11 = bf16[16,104,128]{2,1,0:T(8,128)(2,1)} all-to-all(bf16[16,104,128]{2,1,0:T(8,128)(2,1)S(1)} %broadcast_in_dim.15), channel_id=1, replica_groups=mesh['crop'=8,'z_lo'=4,'x'=4,'z_hi'=4] {'z_lo','x'}, dimensions={0} | all-to-all | bytes 851968 | tf_op jit(solution)/shard_map/all_to_all | solution.py:346
  129.7 2.0 %unpack_sums.1 = (f32[1,128]{1,0:T(1,128)}, f32[1,128]{1,0:T(1,128)}, f32[128,512]{1,0:T(8,128)}, f32[128,512]{1,0:T(8,128)}, f32[512,128]{1,0:T(8,128)}, /*index=5*/f32[64,128]{1,0:T(8,128)}, f32[1,64]{1,0:T(1,128)}) custom-call(bf16[1664,128]{1,0:T(8,128)(2,1)} %bitcast.11), custom_call_target="tpu_custom_call" | custom-call | tf_op jit(solution)/shard_map/unpack_sums/pallas_call | solution.py:350
  (2 shorter events, 0.0 us)
Async XLA Ops:
  7.7 20.5 %collective-permute-start.2 = (bf16[528,128]{1,0:T(8,128)(2,1)}, bf16[528,128]{1,0:T(8,128)(2,1)S(1)}, u32[]{:S(2)}, u32[]{:S(2)}) collective-permute-start(bf16[528,128]{1,0:T(8,128)(2,1)} %get-tuple-element.27), channel_id=1, source_target_pairs={{0,0},{1,16},{2,32},{3,48},{4,4},{5,20},{6,36},{7,52},{8,8},{9,24}... | collective-permute-start | bytes 405512 | tf_op jit(solution)/shard_map/ppermute | solution.py:289
  9.3 18.9 %collective-permute-start.3 = (bf16[528,128]{1,0:T(8,128)(2,1)}, bf16[528,128]{1,0:T(8,128)(2,1)S(1)}, u32[]{:S(2)}, u32[]{:S(2)}) collective-permute-start(bf16[528,128]{1,0:T(8,128)(2,1)} %get-tuple-element.28), channel_id=1, source_target_pairs={{0,4},{1,20},{2,36},{3,52},{4,8},{5,24},{6,40},{7,56},{8,12},{9,28... | collective-permute-start | bytes 405512 | tf_op jit(solution)/shard_map/ppermute | solution.py:289
  19.2 20.7 %collective-permute-start = (bf16[528,128]{1,0:T(8,128)(2,1)}, bf16[528,128]{1,0:T(8,128)(2,1)S(1)}, u32[]{:S(2)}, u32[]{:S(2)}) collective-permute-start(bf16[528,128]{1,0:T(8,128)(2,1)} %get-tuple-element.30), channel_id=1, source_target_pairs={{0,8},{1,24},{2,40},{3,56},{4,12},{5,28},{6,44},{7,60},{8,0},{9,16... | collective-permute-start | bytes 405512 | tf_op jit(solution)/shard_map/ppermute | solution.py:289
  23.8 16.1 %collective-permute-start.1 = (bf16[528,128]{1,0:T(8,128)(2,1)}, bf16[528,128]{1,0:T(8,128)(2,1)S(1)}, u32[]{:S(2)}, u32[]{:S(2)}) collective-permute-start(bf16[528,128]{1,0:T(8,128)(2,1)} %get-tuple-element.31), channel_id=1, source_target_pairs={{0,12},{1,28},{2,44},{3,60},{4,0},{5,16},{6,32},{7,48},{8,4},{9,20... | collective-permute-start | bytes 405512 | tf_op jit(solution)/shard_map/ppermute | solution.py:289
  28.2 0.7 copy-start
  28.9 0.7 copy-start.1
  39.9 0.7 copy-start.2
  40.0 0.7 copy-start.3

commit v3 on v2

--- a/solution.py
+++ b/solution.py
@@ -22,7 +22,8 @@
 SHARE = 104
 PACK = GROUP * SHARE
 GRID_AXES = ("z_lo", "x", "z_hi")
-VMEM_LIMIT = 56 * 1024 * 1024
+VMEM_ALONE = 60 * 1024 * 1024
+VMEM_LIMIT = 36 * 1024 * 1024
 
 
 def dot(a, b, a_dim, b_dim):
@@ -55,8 +56,8 @@
 
 
 def send_kernel(
-    k_ref, pair_ref, gain_ref, bias_ref, w_gate_ref, w_up_ref, w_down_ref, head_t_ref, head_bias_ref,
-    targets_ref, mask_ref, *rest,
+    shift, x_ref, pair_ref, gain_ref, bias_ref, w_gate_ref, w_up_ref, w_down_ref, head_t_ref,
+    head_bias_ref, targets_ref, mask_ref, *rest,
 ):
     wire_refs, (w_gu_ref, half_ref, codes_ref) = rest[:2], rest[2:]
     turn = pl.program_id(0)
@@ -81,7 +82,7 @@
     updated = (rows + jnp.dot(hidden, w_down_ref[...], preferred_element_type=F32)).astype(BF16)
     half_ref[...] = dot(updated, head_twice, 1, 1) + head_bias
     lane = lax.broadcasted_iota(jnp.int32, (SIDE, 128), 1)
-    start = pl.multiple_of(k_ref[turn] * SIDE, SIDE)
+    start = pl.multiple_of(lax.rem(x_ref[0] + shift + turn, 4) * SIDE, SIDE)
 
     def write(wire_ref):
         for j in range(SIDE // 2):
@@ -97,7 +98,7 @@
 
 
 def back_kernel(
-    first, k_ref, pair_ref, gain_ref, bias_ref, w_gate_ref, w_up_ref, w_down_ref, head_t_ref,
+    first, shift, x_ref, pair_ref, gain_ref, bias_ref, w_gate_ref, w_up_ref, w_down_ref, head_t_ref,
     head_bias_ref, targets_ref, mask_ref, wire_a_ref, wire_b_ref, *rest,
 ):
     turn = pl.program_id(0)
@@ -108,15 +109,22 @@
         *acc_ins, _, pack_ref, grad_ref = rest[:7]
         rest = rest[7:]
     (acc_gu, acc_down, acc_head, acc_small, w_gu_ref, normed_s, xhat_s, rstd_s, gate_up_s, hidden_s,
-     updated_s, grad_s, gu_grad_s, codes_s, half_grad_s, grad_t_s) = rest
+     updated_s, grad_s, gu_grad_s, codes_s, half_grad_s, grad_t_s, wire_s, sems) = rest
     accs = (acc_gu, acc_down, acc_head, acc_small)
+    moves = [(wire_a_ref, wire_s.at[0]), (wire_b_ref, wire_s.at[1])]
+    if not first:
+        moves += zip(acc_ins, accs)
+    copies = [pltpu.make_async_copy(a, b, sems.at[n]) for n, (a, b) in enumerate(moves)]
 
     @pl.when(turn == 0)
     def _():
         w_gu_ref[:, :FF] = w_gate_ref[...]
         w_gu_ref[:, FF:] = w_up_ref[...]
-        for n, acc in enumerate(accs):
-            acc[...] = jnp.zeros(acc.shape, F32) if first else acc_ins[n][...]
+        for copy in copies:
+            copy.start()
+        if first:
+            for acc in accs:
+                acc[...] = jnp.zeros(acc.shape, F32)
 
     gain, bias = gain_ref[...], bias_ref[...]
     head_bias = jnp.concatenate([head_bias_ref[...], head_bias_ref[...]], axis=1)
@@ -143,13 +151,19 @@
 
     updated = updated_s[...]
     half = (dot(head_t_ref[...], updated, 1, 1) + head_bias).astype(BF16).astype(F32)
-    wire = jnp.where(turn == 0, wire_a_ref[...].astype(F32), wire_b_ref[...].astype(F32))
+
+    @pl.when(turn == 0)
+    def _():
+        for copy in copies[:2]:
+            copy.wait()
+
+    wire = wire_s[turn].astype(F32)
     mirror = wire[: PAIRS // 2].T
     symmetric = half + jnp.concatenate([mirror[:NB], mirror[NB:]], axis=1)
     symmetric = symmetric - jnp.max(symmetric, axis=0, keepdims=True)
     exped = jnp.exp(symmetric)
     prob = exped / jnp.sum(exped, axis=0, keepdims=True)
-    shift = lax.rem(128 - k_ref[turn] * SIDE, 128)
+    lane_shift = lax.rem(128 - lax.rem(x_ref[0] + 4 - shift - turn, 4) * SIDE, 128)
     codes_s[pl.ds(0, SIDE), :] = targets_ref[...].astype(F32)
     codes_s[pl.ds(SIDE, SIDE), :] = mask_ref[...].astype(F32)
     theirs = wire[PAIRS // 2 :]
@@ -157,8 +171,8 @@
     def line(rows):
         return jnp.concatenate([rows[r : r + 1] for r in range(8)], axis=1)
 
-    own_target = line(spread(codes_s, 0, shift))
-    own_mask = line(spread(codes_s, SIDE, shift))
+    own_target = line(spread(codes_s, 0, lane_shift))
+    own_mask = line(spread(codes_s, SIDE, lane_shift))
     their_target, their_mask = line(theirs[:8]), line(theirs[8:])
     level = lax.broadcasted_iota(jnp.int32, (NB, PAIRS), 0).astype(F32)
     half_grad = (
@@ -207,6 +221,11 @@
         [jnp.broadcast_to(head_bias_sum, (NB, 128)), jnp.zeros((NB, 128), F32)], axis=0
     ).T[:1]
     small = jnp.concatenate([gain_sum, bias_sum, head_bias_row, jnp.zeros((5, 128), F32)], axis=0)
+    @pl.when(turn == 0)
+    def _():
+        for copy in copies[2:]:
+            copy.wait()
+
     acc_gu[...] += gu_sum
     acc_down[...] += down_sum
     acc_head[...] += head_sum
@@ -252,22 +271,26 @@
     pair, norm_gain, norm_bias, w_gate, w_up, w_down, head_weight, head_bias, targets, mask
 ):
     length = SIDE * 16
-    place = lax.axis_index("x")
+    place = lax.axis_index("x")[None]
     params = pltpu.CompilerParams(vmem_limit_bytes=VMEM_LIMIT)
     common = (
         pair, norm_gain[None], norm_bias[None], w_gate, w_up, w_down, head_weight.T, head_bias[None],
         targets, mask,
     )
-    block = pl.BlockSpec((SIDE, SIDE, C), lambda i, k: (0, k[i], 0))
-    common_specs = [block] + [full(a.shape) for a in common[1:]]
-
-    def send(shift, blocks):
+    rest_specs = [full(a.shape) for a in common[1:]]
+
+    def block(shift, sign):
+        return pl.BlockSpec(
+            (SIDE, SIDE, C), lambda i, x: (0, lax.rem(x[0] + 4 + sign * (shift + i), 4), 0)
+        )
+
+    def send(shift, place):
         wires = pl.pallas_call(
-            send_kernel,
+            functools.partial(send_kernel, shift),
             grid_spec=pltpu.PrefetchScalarGridSpec(
                 num_scalar_prefetch=1,
                 grid=(2,),
-                in_specs=common_specs,
+                in_specs=[block(shift, 1)] + rest_specs,
                 out_specs=[full((WIRE, 128))] * 2,
                 scratch_shapes=[
                     pltpu.VMEM((C, 2 * FF), BF16),
@@ -276,9 +299,11 @@
                 ],
             ),
             out_shape=[jax.ShapeDtypeStruct((WIRE, 128), BF16)] * 2,
-            compiler_params=params,
+            compiler_params=pltpu.CompilerParams(
+                vmem_limit_bytes=VMEM_LIMIT if shift else VMEM_ALONE
+            ),
             name="forward_send",
-        )(blocks, *common)
+        )(place, *common)
         routes = [
             [
                 ((a * 4 + x) * 4 + b, (b * 4 + (x + shift + n) % 4) * 4 + a)
@@ -288,9 +313,8 @@
         ]
         return wires, [lax.ppermute(wire, GRID_AXES, route) for wire, route in zip(wires, routes)]
 
-    near = lax.rem(place + jnp.arange(4, dtype=jnp.int32), 4)
-    early, wires = send(0, near[:2])
-    later, _ = lax.optimization_barrier((near[2:], early))
+    early, wires = send(0, place)
+    later, _ = lax.optimization_barrier((place, early))
     wires = wires + send(2, later)[1]
     sums = [
         jax.ShapeDtypeStruct((C, 2 * FF), F32),
@@ -298,21 +322,19 @@
         jax.ShapeDtypeStruct((NB, C), F32),
         jax.ShapeDtypeStruct((8, C), F32),
     ]
-    sum_specs = [full(a.shape) for a in sums]
+    anywhere = pl.BlockSpec(memory_space=pl.ANY)
     state = ()
     for first in (True, False):
         shift = 0 if first else 2
         out_shape = sums if first else [jax.ShapeDtypeStruct((PACK, 128), BF16)]
         out_specs = [full(a.shape) for a in out_shape]
         state = pl.pallas_call(
-            functools.partial(back_kernel, first),
+            functools.partial(back_kernel, first, shift),
             grid_spec=pltpu.PrefetchScalarGridSpec(
                 num_scalar_prefetch=1,
                 grid=(2,),
-                in_specs=common_specs
-                + [full((WIRE, 128))] * 2
-                + ([] if first else sum_specs + [pl.BlockSpec(memory_space=pl.ANY)]),
-                out_specs=out_specs + [block],
+                in_specs=[block(shift, -1)] + rest_specs + [anywhere] * (2 if first else 7),
+                out_specs=out_specs + [block(shift, -1)],
                 scratch_shapes=[pltpu.VMEM(a.shape, F32) for a in sums]
                 + [
                     pltpu.VMEM((C, 2 * FF), BF16),
@@ -327,6 +349,8 @@
                     pltpu.VMEM((2 * SIDE, 128), F32),
                     pltpu.VMEM((NB, PAIRS), BF16),
                     pltpu.VMEM((C, PAIRS), BF16),
+                    pltpu.VMEM((2, WIRE, 128), BF16),
+                    pltpu.SemaphoreType.DMA((6,)),
                 ],
             ),
             out_shape=out_shape + [jax.ShapeDtypeStruct(pair.shape, BF16)],
@@ -334,8 +358,7 @@
             compiler_params=params,
             name="backward_blocks",
         )(
-            lax.rem(place + 4 - shift - jnp.arange(2, dtype=jnp.int32), 4), *common,
-            wires[shift], wires[shift + 1], *state,
+            place, *common, wires[shift], wires[shift + 1], *state,
         )
     pack, pair_grad = state
 

time: 132 us -> 123 us (0.932)
  Pallas kernels: 35.9 us -> 30.5 us
  local copies, waits for them, and re-layouts: 2.61 us -> 0.1 us
    pallas_call x4, Pallas kernels: 33.9 us -> 29.5 us  [the longest x2 19.6 us: on_device(): pl.pallas_call(functools.partial(back_kernel, first, shift), grid_spec=pl...]
    all_to_all x1, blocking collectives: 45.3 us -> 43.1 us  [on_device(): lax.all_to_all(pack.reshape(GROUP, SHARE, 128), ('z_lo', 'x'), 0, 0)]
    unnamed x8 -> x20, local copies, waits for them, and re-layouts: 1.97 us -> 0.04 us
    all_gather x1, blocking collectives: 17.6 us -> 19.2 us  [on_device(): shares = lax.all_gather(share, 'z_hi')]
  transfers between devices with their start and end apart: 4 -> 4, of which waited for: 0 -> 0; matrix products, arithmetic and copies ran while one was open for 1% -> 0% of each run, Pallas kernels for 13% -> 11%
where the time goes in v3:
time: 123 us
  blocking collectives  77.8 us (63%)
  Pallas kernels  30.5 us (25%)
  starting transfers between devices  13.2 us (11%)
    all_to_all x1, blocking collectives, on_device(): lax.all_to_all(pack.reshape(GROUP, SHARE, 128), ('z_lo', 'x'), 0, 0)  43.1 us
    pallas_call x2, Pallas kernels, on_device(): pl.pallas_call(functools.partial(back_kernel, first, shift), grid_spec=pl...  19.6 us
    all_gather x1, blocking collectives, on_device(): shares = lax.all_gather(share, 'z_hi')  19.2 us
    all_to_all x1, blocking collectives, on_device(): lax.all_to_all(jnp.broadcast_to(share, (GROUP, SHARE, 128)), ('z_lo', 'x'...  15.5 us
    ppermute x4, starting transfers between devices, send(): lax.ppermute(wire, GRID_AXES, route)  13.2 us
    pallas_call x2, Pallas kernels, send(): pl.pallas_call(functools.partial(send_kernel, shift), grid_spec=pltpu.Pre...  9.92 us
  transfers between devices with their start and end apart: 4, of which 0 were waited for; matrix products, arithmetic and copies ran while one was open for 0% of the time, Pallas kernels for 11%

profile of v3, /device:TPU:8, one launch (start us, length us, event | category | flops | bytes accessed | tf_op | source)
XLA Modules:
  0.0 122.5 jit_solution(18111536423302821539)
XLA Ops:
  0.6 0.0 copy-start
  0.7 0.0 copy-start.1
  0.7 0.0 copy-start.2
  0.7 0.0 copy-start.3
  0.7 0.0 copy-start.4
  0.7 0.0 copy-start.5
  0.7 0.0 copy-start.6
  0.7 5.9 %forward_send.2 = (bf16[528,128]{1,0:T(8,128)(2,1)}, bf16[528,128]{1,0:T(8,128)(2,1)}) custom-call(s32[1]{0:T(128)} %bitcast.x_ref, bf16[32,128,128]{2,1,0:T(8,128)(2,1)} %pair_ref.7, f32[1,128]{1,0:T(1,128)} %bitcast.18, f32[1,128]{1,0:T(1,128)} %bitcast.22, bf16[128,512]{1,0:T(8,128)(2,1)} %w_gate_ref.7, bf16[128,512]{1,0:T(8,128)(2,1)} %w_up_ref.7, ...), custom_call_target="tpu_custom_call" | custom-call | tf_op jit(solution)/shard_map/forward_send/pallas_call | solution.py:288
  6.6 0.0 copy-start.7
  6.6 0.0 copy-start.8
  6.6 0.0 copy-start.9
  6.6 1.7 %collective-permute-start.2 = (bf16[528,128]{1,0:T(8,128)(2,1)}, bf16[528,128]{1,0:T(8,128)(2,1)S(1)}, u32[]{:S(2)}, u32[]{:S(2)}) collective-permute-start(bf16[528,128]{1,0:T(8,128)(2,1)} %get-tuple-element.27), channel_id=1, source_target_pairs={{0,0},{1,16},{2,32},{3,48},{4,4},{5,20},{6,36},{7,52},{8,8},{9,24}... | collective-permute-start | bytes 405512 | tf_op jit(solution)/shard_map/ppermute | solution.py:314
  8.3 3.4 %collective-permute-start.3 = (bf16[528,128]{1,0:T(8,128)(2,1)}, bf16[528,128]{1,0:T(8,128)(2,1)S(1)}, u32[]{:S(2)}, u32[]{:S(2)}) collective-permute-start(bf16[528,128]{1,0:T(8,128)(2,1)} %get-tuple-element.28), channel_id=1, source_target_pairs={{0,4},{1,20},{2,36},{3,52},{4,8},{5,24},{6,40},{7,56},{8,12},{9,28... | collective-permute-start | bytes 405512 | tf_op jit(solution)/shard_map/ppermute | solution.py:314
  11.7 0.0 copy-done
  11.7 0.0 copy-done.1
  11.7 0.0 copy-done.2
  11.7 0.0 copy-done.3
  11.8 0.0 copy-done.4
  11.8 0.0 copy-done.5
  11.8 0.0 copy-done.6
  11.8 0.0 copy-done.7
  11.8 0.0 copy-done.8
  11.8 0.0 copy-done.9
  11.8 4.0 %forward_send.3 = (bf16[528,128]{1,0:T(8,128)(2,1)S(1)}, bf16[528,128]{1,0:T(8,128)(2,1)S(1)}) custom-call(s32[1]{0:T(128)} %bitcast.x_ref, bf16[32,128,128]{2,1,0:T(8,128)(2,1)S(1)} %copy-done, f32[1,128]{1,0:T(1,128)S(1)} %bitcast.19, f32[1,128]{1,0:T(1,128)S(1)} %bitcast.23, bf16[128,512]{1,0:T(8,128)(2,1)S(1)} %copy-done.1, ...), custom_call_target="tpu_custom_call" | custom-call | tf_op jit(solution)/shard_map/forward_send/pallas_call | solution.py:288
  15.8 4.6 %collective-permute-start = (bf16[528,128]{1,0:T(8,128)(2,1)S(1)}, bf16[528,128]{1,0:T(8,128)(2,1)S(1)}, u32[]{:S(2)}, u32[]{:S(2)}) collective-permute-start(bf16[528,128]{1,0:T(8,128)(2,1)S(1)} %get-tuple-element.30), channel_id=1, source_target_pairs={{0,8},{1,24},{2,40},{3,56},{4,12},{5,28},{6,44},{7,60},{8,0},{9,16... | collective-permute-start | bytes 405512 | tf_op jit(solution)/shard_map/ppermute | solution.py:314
  20.5 3.5 %collective-permute-start.1 = (bf16[528,128]{1,0:T(8,128)(2,1)S(1)}, bf16[528,128]{1,0:T(8,128)(2,1)S(1)}, u32[]{:S(2)}, u32[]{:S(2)}) collective-permute-start(bf16[528,128]{1,0:T(8,128)(2,1)S(1)} %get-tuple-element.31), channel_id=1, source_target_pairs={{0,12},{1,28},{2,44},{3,60},{4,0},{5,16},{6,32},{7,48},{8,4},{9,20... | collective-permute-start | bytes 405512 | tf_op jit(solution)/shard_map/ppermute | solution.py:314
  24.0 0.0 collective-permute-done.2.wire_a_ref
  24.0 0.0 collective-permute-done.3.wire_b_ref
  24.0 9.7 %backward_blocks.2 = (f32[128,1024]{1,0:T(8,128)S(1)}, f32[128,512]{1,0:T(8,128)S(1)}, f32[64,128]{1,0:T(8,128)S(1)}, f32[8,128]{1,0:T(8,128)S(1)}, bf16[32,128,128]{2,1,0:T(8,128)(2,1)}) custom-call(s32[1]{0:T(128)} %bitcast.x_ref, bf16[32,128,128]{2,1,0:T(8,128)(2,1)S(1)} %copy-done, f32[1,128]{1,0:T(1,128)S(1)} %bitcast.20, f32[1,128]{1,0:T(1,128)S(1)} %bitcast.24, ...), custom_call_target="tpu_custom_call" | custom-call | tf_op jit(solution)/shard_map/backward_blocks/pallas_call | solution.py:331
  33.7 0.0 collective-permute-done.wire_a_ref
  33.7 0.0 collective-permute-done.1.wire_b_ref
  33.8 9.9 %backward_blocks.3 = (bf16[1664,128]{1,0:T(8,128)(2,1)S(1)}, bf16[32,128,128]{2,1,0:T(8,128)(2,1)}) custom-call(s32[1]{0:T(128)} %bitcast.x_ref, bf16[32,128,128]{2,1,0:T(8,128)(2,1)S(1)} %copy-done, f32[1,128]{1,0:T(1,128)S(1)} %bitcast.21, f32[1,128]{1,0:T(1,128)S(1)} %bitcast.25, ...), custom_call_target="tpu_custom_call", output_to_operand_aliasing={{1}: (17, {})} | custom-call | tf_op jit(solution)/shard_map/backward_blocks/pallas_call | solution.py:331
  43.7 43.1 %all_to_all.10 = bf16[16,104,128]{2,1,0:T(8,128)(2,1)S(1)} all-to-all(bf16[16,104,128]{2,1,0:T(8,128)(2,1)S(1)} %bitcast.13), channel_id=1, replica_groups=mesh['crop'=8,'z_lo'=4,'x'=4,'z_hi'=4] {'z_lo','x'}, dimensions={0} | all-to-all | bytes 851968 | tf_op jit(solution)/shard_map/all_to_all | solution.py:365
  86.8 0.1 reduce_sum.24
  86.8 19.2 %all-gather = bf16[416,128]{1,0:T(8,128)(2,1)S(1)} all-gather(bf16[104,128]{1,0:T(8,128)(2,1)S(1)} %reduce_sum.24), channel_id=2, replica_groups=mesh['crop'=8,'z_lo'=4,'x'=4,'z_hi'=4] {'z_hi'}, dimensions={0}, use_global_device_ids=true | all-gather | bytes 133120 | tf_op jit(solution)/shard_map/all_gather | solution.py:367
  106.0 0.1 broadcast_in_dim.19
  106.1 15.5 %all_to_all.11 = bf16[16,104,128]{2,1,0:T(8,128)(2,1)S(1)} all-to-all(bf16[16,104,128]{2,1,0:T(8,128)(2,1)S(1)} %broadcast_in_dim.19), channel_id=1, replica_groups=mesh['crop'=8,'z_lo'=4,'x'=4,'z_hi'=4] {'z_lo','x'}, dimensions={0} | all-to-all | bytes 851968 | tf_op jit(solution)/shard_map/all_to_all | solution.py:369
  121.6 1.0 unpack_sums.1
  (1 shorter events, 0.0 us)
Async XLA Ops:
  0.6 11.1 %copy-start = (bf16[32,128,128]{2,1,0:T(8,128)(2,1)S(1)}, bf16[32,128,128]{2,1,0:T(8,128)(2,1)}, u32[]{:S(2)}) copy-start(bf16[32,128,128]{2,1,0:T(8,128)(2,1)} %pair_ref.7) | copy-start | bytes 3145732
  0.7 11.1 %copy-start.1 = (bf16[128,512]{1,0:T(8,128)(2,1)S(1)}, bf16[128,512]{1,0:T(8,128)(2,1)}, u32[]{:S(2)}) copy-start(bf16[128,512]{1,0:T(8,128)(2,1)} %w_gate_ref.7) | copy-start | bytes 393220
  0.7 11.1 %copy-start.2 = (bf16[128,512]{1,0:T(8,128)(2,1)S(1)}, bf16[128,512]{1,0:T(8,128)(2,1)}, u32[]{:S(2)}) copy-start(bf16[128,512]{1,0:T(8,128)(2,1)} %w_up_ref.7) | copy-start | bytes 393220
  0.7 11.1 %copy-start.3 = (bf16[512,128]{1,0:T(8,128)(2,1)S(1)}, bf16[512,128]{1,0:T(8,128)(2,1)}, u32[]{:S(2)}) copy-start(bf16[512,128]{1,0:T(8,128)(2,1)} %w_down_ref.7) | copy-start | bytes 393220
  0.7 11.1 %copy-start.4 = (bf16[128,64]{0,1:T(8,128)(2,1)S(1)}, bf16[128,64]{0,1:T(8,128)(2,1)}, u32[]{:S(2)}) copy-start(bf16[128,64]{0,1:T(8,128)(2,1)} %param.16) | copy-start | bytes 49156
  0.7 11.1 %copy-start.5 = (s32[32,128]{1,0:T(8,128)S(1)}, s32[32,128]{1,0:T(8,128)}, u32[]{:S(2)}) copy-start(s32[32,128]{1,0:T(8,128)} %targets_ref.7) | copy-start | bytes 49156
  0.7 11.1 %copy-start.6 = (s32[32,128]{1,0:T(8,128)S(1)}, s32[32,128]{1,0:T(8,128)}, u32[]{:S(2)}) copy-start(s32[32,128]{1,0:T(8,128)} %mask_ref.7) | copy-start | bytes 49156
  6.6 5.2 %copy-start.7 = (f32[128]{0:T(128)S(1)}, f32[128]{0:T(128)}, u32[]{:S(2)}) copy-start(f32[128]{0:T(128)} %param.11) | copy-start | bytes 1540
  6.6 5.2 %copy-start.8 = (f32[128]{0:T(128)S(1)}, f32[128]{0:T(128)}, u32[]{:S(2)}) copy-start(f32[128]{0:T(128)} %param.12) | copy-start | bytes 1540
  6.6 5.2 %copy-start.9 = (f32[64]{0:T(128)S(1)}, f32[64]{0:T(128)}, u32[]{:S(2)}) copy-start(f32[64]{0:T(128)} %param.17) | copy-start | bytes 772
  6.6 17.4 %collective-permute-start.2 = (bf16[528,128]{1,0:T(8,128)(2,1)}, bf16[528,128]{1,0:T(8,128)(2,1)S(1)}, u32[]{:S(2)}, u32[]{:S(2)}) collective-permute-start(bf16[528,128]{1,0:T(8,128)(2,1)} %get-tuple-element.27), channel_id=1, source_target_pairs={{0,0},{1,16},{2,32},{3,48},{4,4},{5,20},{6,36},{7,52},{8,8},{9,24}... | collective-permute-start | bytes 405512 | tf_op jit(solution)/shard_map/ppermute | solution.py:314
  8.3 15.7 %collective-permute-start.3 = (bf16[528,128]{1,0:T(8,128)(2,1)}, bf16[528,128]{1,0:T(8,128)(2,1)S(1)}, u32[]{:S(2)}, u32[]{:S(2)}) collective-permute-start(bf16[528,128]{1,0:T(8,128)(2,1)} %get-tuple-element.28), channel_id=1, source_target_pairs={{0,4},{1,20},{2,36},{3,52},{4,8},{5,24},{6,40},{7,56},{8,12},{9,28... | collective-permute-start | bytes 405512 | tf_op jit(solution)/shard_map/ppermute | solution.py:314
  15.8 17.9 %collective-permute-start = (bf16[528,128]{1,0:T(8,128)(2,1)S(1)}, bf16[528,128]{1,0:T(8,128)(2,1)S(1)}, u32[]{:S(2)}, u32[]{:S(2)}) collective-permute-start(bf16[528,128]{1,0:T(8,128)(2,1)S(1)} %get-tuple-element.30), channel_id=1, source_target_pairs={{0,8},{1,24},{2,40},{3,56},{4,12},{5,28},{6,44},{7,60},{8,0},{9,16... | collective-permute-start | bytes 405512 | tf_op jit(solution)/shard_map/ppermute | solution.py:314
  20.5 13.3 %collective-permute-start.1 = (bf16[528,128]{1,0:T(8,128)(2,1)S(1)}, bf16[528,128]{1,0:T(8,128)(2,1)S(1)}, u32[]{:S(2)}, u32[]{:S(2)}) collective-permute-start(bf16[528,128]{1,0:T(8,128)(2,1)S(1)} %get-tuple-element.31), channel_id=1, source_target_pairs={{0,12},{1,28},{2,44},{3,60},{4,0},{5,16},{6,32},{7,48},{8,4},{9,20... | collective-permute-start | bytes 405512 | tf_op jit(solution)/shard_map/ppermute | solution.py:314

commit v4 on v3

--- a/solution.py
+++ b/solution.py
@@ -21,6 +21,8 @@
 GROUP = 16
 SHARE = 104
 PACK = GROUP * SHARE
+SENDS = ((0, 1), (1, 1), (2, 2))
+BACKS = ((0, 1), (1, 1), (2, 1), (3, 1))
 GRID_AXES = ("z_lo", "x", "z_hi")
 VMEM_ALONE = 60 * 1024 * 1024
 VMEM_LIMIT = 36 * 1024 * 1024
@@ -59,7 +61,7 @@
     shift, x_ref, pair_ref, gain_ref, bias_ref, w_gate_ref, w_up_ref, w_down_ref, head_t_ref,
     head_bias_ref, targets_ref, mask_ref, *rest,
 ):
-    wire_refs, (w_gu_ref, half_ref, codes_ref) = rest[:2], rest[2:]
+    *wire_refs, w_gu_ref, half_ref, codes_ref = rest
     turn = pl.program_id(0)
 
     @pl.when(turn == 0)
@@ -93,25 +95,28 @@
             [spread(codes_ref, start, 0), spread(codes_ref, start, 96)], axis=0
         ).astype(BF16)
 
-    for n in range(2):
-        pl.when(turn == n)(functools.partial(write, wire_refs[n]))
+    for n, wire_ref in enumerate(wire_refs):
+        pl.when(turn == n)(functools.partial(write, wire_ref))
 
 
 def back_kernel(
-    first, shift, x_ref, pair_ref, gain_ref, bias_ref, w_gate_ref, w_up_ref, w_down_ref, head_t_ref,
-    head_bias_ref, targets_ref, mask_ref, wire_a_ref, wire_b_ref, *rest,
+    shift, count, x_ref, pair_ref, gain_ref, bias_ref, w_gate_ref, w_up_ref, w_down_ref, head_t_ref,
+    head_bias_ref, targets_ref, mask_ref, *rest,
 ):
     turn = pl.program_id(0)
-    if first:
-        *acc_outs, grad_ref = rest[:5]
-        rest = rest[5:]
+    first, last = shift == 0, shift + count == 4
+    wire_refs, rest = rest[:count], rest[count:]
+    if not first:
+        acc_ins, rest = rest[:4], rest[5:]
+    if last:
+        pack_ref, rest = rest[0], rest[1:]
     else:
-        *acc_ins, _, pack_ref, grad_ref = rest[:7]
-        rest = rest[7:]
+        acc_outs, rest = rest[:4], rest[4:]
+    grad_ref, *rest = rest
     (acc_gu, acc_down, acc_head, acc_small, w_gu_ref, normed_s, xhat_s, rstd_s, gate_up_s, hidden_s,
      updated_s, grad_s, gu_grad_s, codes_s, half_grad_s, grad_t_s, wire_s, sems) = rest
     accs = (acc_gu, acc_down, acc_head, acc_small)
-    moves = [(wire_a_ref, wire_s.at[0]), (wire_b_ref, wire_s.at[1])]
+    moves = [(wire_ref, wire_s.at[n]) for n, wire_ref in enumerate(wire_refs)]
     if not first:
         moves += zip(acc_ins, accs)
     copies = [pltpu.make_async_copy(a, b, sems.at[n]) for n, (a, b) in enumerate(moves)]
@@ -154,7 +159,7 @@
 
     @pl.when(turn == 0)
     def _():
-        for copy in copies[:2]:
+        for copy in copies[:count]:
             copy.wait()
 
     wire = wire_s[turn].astype(F32)
@@ -223,7 +228,7 @@
     small = jnp.concatenate([gain_sum, bias_sum, head_bias_row, jnp.zeros((5, 128), F32)], axis=0)
     @pl.when(turn == 0)
     def _():
-        for copy in copies[2:]:
+        for copy in copies[count:]:
             copy.wait()
 
     acc_gu[...] += gu_sum
@@ -231,9 +236,9 @@
     acc_head[...] += head_sum
     acc_small[...] += small
 
-    @pl.when(turn == 1)
+    @pl.when(turn == count - 1)
     def _():
-        if first:
+        if not last:
             for acc, out in zip(accs, acc_outs):
                 out[...] = acc[...]
         else:
@@ -284,21 +289,21 @@
             (SIDE, SIDE, C), lambda i, x: (0, lax.rem(x[0] + 4 + sign * (shift + i), 4), 0)
         )
 
-    def send(shift, place):
+    def send(shift, count, place):
         wires = pl.pallas_call(
             functools.partial(send_kernel, shift),
             grid_spec=pltpu.PrefetchScalarGridSpec(
                 num_scalar_prefetch=1,
-                grid=(2,),
+                grid=(count,),
                 in_specs=[block(shift, 1)] + rest_specs,
-                out_specs=[full((WIRE, 128))] * 2,
+                out_specs=[full((WIRE, 128))] * count,
                 scratch_shapes=[
                     pltpu.VMEM((C, 2 * FF), BF16),
                     pltpu.VMEM((PAIRS, 128), F32),
                     pltpu.VMEM((128, 128), F32),
                 ],
             ),
-            out_shape=[jax.ShapeDtypeStruct((WIRE, 128), BF16)] * 2,
+            out_shape=[jax.ShapeDtypeStruct((WIRE, 128), BF16)] * count,
             compiler_params=pltpu.CompilerParams(
                 vmem_limit_bytes=VMEM_LIMIT if shift else VMEM_ALONE
             ),
@@ -309,13 +314,15 @@
                 ((a * 4 + x) * 4 + b, (b * 4 + (x + shift + n) % 4) * 4 + a)
                 for a in range(4) for x in range(4) for b in range(4)
             ]
-            for n in range(2)
+            for n in range(count)
         ]
         return wires, [lax.ppermute(wire, GRID_AXES, route) for wire, route in zip(wires, routes)]
 
-    early, wires = send(0, place)
-    later, _ = lax.optimization_barrier((place, early))
-    wires = wires + send(2, later)[1]
+    wires, turn = [], place
+    for shift, count in SENDS:
+        sent, arrived = send(shift, count, turn)
+        turn, _ = lax.optimization_barrier((place, sent))
+        wires += arrived
     sums = [
         jax.ShapeDtypeStruct((C, 2 * FF), F32),
         jax.ShapeDtypeStruct((C, FF), F32),
@@ -324,16 +331,18 @@
     ]
     anywhere = pl.BlockSpec(memory_space=pl.ANY)
     state = ()
-    for first in (True, False):
-        shift = 0 if first else 2
-        out_shape = sums if first else [jax.ShapeDtypeStruct((PACK, 128), BF16)]
+    for shift, count in BACKS:
+        first, last = shift == 0, shift + count == 4
+        out_shape = sums if not last else [jax.ShapeDtypeStruct((PACK, 128), BF16)]
         out_specs = [full(a.shape) for a in out_shape]
         state = pl.pallas_call(
-            functools.partial(back_kernel, first, shift),
+            functools.partial(back_kernel, shift, count),
             grid_spec=pltpu.PrefetchScalarGridSpec(
                 num_scalar_prefetch=1,
-                grid=(2,),
-                in_specs=[block(shift, -1)] + rest_specs + [anywhere] * (2 if first else 7),
+                grid=(count,),
+                in_specs=[block(shift, -1)]
+                + rest_specs
+                + [anywhere] * (count if first else count + 5),
                 out_specs=out_specs + [block(shift, -1)],
                 scratch_shapes=[pltpu.VMEM(a.shape, F32) for a in sums]
                 + [
@@ -349,16 +358,16 @@
                     pltpu.VMEM((2 * SIDE, 128), F32),
                     pltpu.VMEM((NB, PAIRS), BF16),
                     pltpu.VMEM((C, PAIRS), BF16),
-                    pltpu.VMEM((2, WIRE, 128), BF16),
-                    pltpu.SemaphoreType.DMA((6,)),
+                    pltpu.VMEM((count, WIRE, 128), BF16),
+                    pltpu.SemaphoreType.DMA((count if first else count + 4,)),
                 ],
             ),
             out_shape=out_shape + [jax.ShapeDtypeStruct(pair.shape, BF16)],
-            input_output_aliases={} if first else {17: 1},
+            input_output_aliases={} if first else {11 + count + 4: len(out_shape)},
             compiler_params=params,
             name="backward_blocks",
         )(
-            place, *common, wires[shift], wires[shift + 1], *state,
+            place, *common, *wires[shift : shift + count], *state,
         )
     pack, pair_grad = state
 

time: 123 us -> 119 us (0.967)
  blocking collectives: 77.8 us -> 73.6 us
    all_to_all x1, blocking collectives: 43.1 us -> 39.8 us  [on_device(): lax.all_to_all(pack.reshape(GROUP, SHARE, 128), ('z_lo', 'x'), 0, 0)]
    pallas_call x2 -> x4, Pallas kernels: 19.6 us -> 20.1 us  [on_device(): pl.pallas_call(functools.partial(back_kernel, shift, count), grid_spec=pl...]
    pallas_call x2 -> x3, Pallas kernels: 9.92 us -> 9.52 us  [send(): pl.pallas_call(functools.partial(send_kernel, shift), grid_spec=pltpu.Pre...]
  transfers between devices with their start and end apart: 4 -> 4, of which waited for: 0 -> 0; matrix products, arithmetic and copies ran while one was open for 0% -> 0% of each run, Pallas kernels for 11% -> 18%
where the time goes in v4:
time: 119 us; the launch traced here: 118 us
  blocking collectives  73.6 us (62%)
  Pallas kernels  30.6 us (26%)
  starting transfers between devices  13.1 us (11%)
    all_to_all x1, blocking collectives, on_device(): lax.all_to_all(pack.reshape(GROUP, SHARE, 128), ('z_lo', 'x'), 0, 0)  39.8 us
    pallas_call x4, Pallas kernels, on_device(): pl.pallas_call(functools.partial(back_kernel, shift, count), grid_spec=pl...  20.1 us
    all_gather x1, blocking collectives, on_device(): shares = lax.all_gather(share, 'z_hi')  18.2 us
    all_to_all x1, blocking collectives, on_device(): lax.all_to_all(jnp.broadcast_to(share, (GROUP, SHARE, 128)), ('z_lo', 'x'...  15.5 us
    ppermute x4, starting transfers between devices, send(): lax.ppermute(wire, GRID_AXES, route)  13.1 us
    pallas_call x3, Pallas kernels, send(): pl.pallas_call(functools.partial(send_kernel, shift), grid_spec=pltpu.Pre...  9.52 us
  transfers between devices with their start and end apart: 4, of which 0 were waited for; matrix products, arithmetic and copies ran while one was open for 0% of the time, Pallas kernels for 18%

profile of v4, /device:TPU:8, one launch (start us, length us, event | category | flops | bytes accessed | tf_op | source)
XLA Modules:
  0.0 118.4 jit_solution(3424932780378652728)
XLA Ops:
  0.6 0.0 copy-start
  0.7 0.0 copy-start.1
  0.7 0.0 copy-start.2
  0.7 0.0 copy-start.3
  0.7 0.0 copy-start.4
  0.7 0.0 copy-start.5
  0.7 0.0 copy-start.6
  0.7 0.0 copy-start.7
  0.7 0.0 copy-start.8
  0.7 0.0 copy-start.9
  0.7 3.7 %forward_send.3 = bf16[528,128]{1,0:T(8,128)(2,1)} custom-call(s32[1]{0:T(128)} %bitcast.x_ref, bf16[32,128,128]{2,1,0:T(8,128)(2,1)} %pair_ref.13, f32[1,128]{1,0:T(1,128)} %bitcast.21, f32[1,128]{1,0:T(1,128)} %bitcast.28, bf16[128,512]{1,0:T(8,128)(2,1)} %w_gate_ref.13, bf16[128,512]{1,0:T(8,128)(2,1)} %w_up_ref.13, bf16[512,128]{1,0:T(8,128)(2,1)} %w_down_ref.13, ...), custom_call_target="tpu_custom_call" | custom-call | tf_op jit(solution)/shard_map/forward_send/pallas_call | solution.py:293
  4.4 1.6 %collective-permute-start.3 = (bf16[528,128]{1,0:T(8,128)(2,1)}, bf16[528,128]{1,0:T(8,128)(2,1)S(1)}, u32[]{:S(2)}, u32[]{:S(2)}) collective-permute-start(bf16[528,128]{1,0:T(8,128)(2,1)} %forward_send.3), channel_id=1, source_target_pairs={{0,0},{1,16},{2,32},{3,48},{4,4},{5,20},{6,36},{7,52},{8,8},{9,24}... | collective-permute-start | bytes 405512 | tf_op jit(solution)/shard_map/ppermute | solution.py:319
  6.0 0.0 copy-done
  6.0 0.0 copy-done.1
  6.0 0.0 copy-done.2
  6.0 0.0 copy-done.3
  6.0 0.0 copy-done.4
  6.0 0.0 copy-done.5
  6.0 0.0 copy-done.6
  6.0 0.0 copy-done.7
  6.0 0.0 copy-done.8
  6.0 0.0 copy-done.9
  6.0 1.8 %forward_send.4 = bf16[528,128]{1,0:T(8,128)(2,1)S(1)} custom-call(s32[1]{0:T(128)} %bitcast.x_ref, bf16[32,128,128]{2,1,0:T(8,128)(2,1)S(1)} %copy-done, f32[1,128]{1,0:T(1,128)S(1)} %bitcast.22, f32[1,128]{1,0:T(1,128)S(1)} %bitcast.29, bf16[128,512]{1,0:T(8,128)(2,1)S(1)} %copy-done.1, bf16[128,512]{1,0:T(8,128)(2,1)S(1)} %copy-done.2, ...), custom_call_target="tpu_custom_call" | custom-call | tf_op jit(solution)/shard_map/forward_send/pallas_call | solution.py:293
  7.9 3.4 %collective-permute-start.2 = (bf16[528,128]{1,0:T(8,128)(2,1)S(1)}, bf16[528,128]{1,0:T(8,128)(2,1)S(1)}, u32[]{:S(2)}, u32[]{:S(2)}) collective-permute-start(bf16[528,128]{1,0:T(8,128)(2,1)S(1)} %forward_send.4), channel_id=1, source_target_pairs={{0,4},{1,20},{2,36},{3,52},{4,8},{5,24},{6,40},{7,56},{8,12},{9,28... | collective-permute-start | bytes 405512 | tf_op jit(solution)/shard_map/ppermute | solution.py:319
  11.3 4.0 %forward_send.5 = (bf16[528,128]{1,0:T(8,128)(2,1)S(1)}, bf16[528,128]{1,0:T(8,128)(2,1)S(1)}) custom-call(s32[1]{0:T(128)} %bitcast.x_ref, bf16[32,128,128]{2,1,0:T(8,128)(2,1)S(1)} %copy-done, f32[1,128]{1,0:T(1,128)S(1)} %bitcast.23, f32[1,128]{1,0:T(1,128)S(1)} %bitcast.30, bf16[128,512]{1,0:T(8,128)(2,1)S(1)} %copy-done.1, ...), custom_call_target="tpu_custom_call" | custom-call | tf_op jit(solution)/shard_map/forward_send/pallas_call | solution.py:293
  15.3 4.6 %collective-permute-start.1 = (bf16[528,128]{1,0:T(8,128)(2,1)S(1)}, bf16[528,128]{1,0:T(8,128)(2,1)S(1)}, u32[]{:S(2)}, u32[]{:S(2)}) collective-permute-start(bf16[528,128]{1,0:T(8,128)(2,1)S(1)} %get-tuple-element.39), channel_id=1, source_target_pairs={{0,8},{1,24},{2,40},{3,56},{4,12},{5,28},{6,44},{7,60},{8,0},{9,16... | collective-permute-start | bytes 405512 | tf_op jit(solution)/shard_map/ppermute | solution.py:319
  20.0 3.5 %collective-permute-start = (bf16[528,128]{1,0:T(8,128)(2,1)S(1)}, bf16[528,128]{1,0:T(8,128)(2,1)S(1)}, u32[]{:S(2)}, u32[]{:S(2)}) collective-permute-start(bf16[528,128]{1,0:T(8,128)(2,1)S(1)} %get-tuple-element.38), channel_id=1, source_target_pairs={{0,12},{1,28},{2,44},{3,60},{4,0},{5,16},{6,32},{7,48},{8,4},{9,20... | collective-permute-start | bytes 405512 | tf_op jit(solution)/shard_map/ppermute | solution.py:319
  23.5 0.0 collective-permute-done.3.rest_0_
  23.5 4.8 %backward_blocks.4 = (f32[128,1024]{1,0:T(8,128)S(1)}, f32[128,512]{1,0:T(8,128)S(1)}, f32[64,128]{1,0:T(8,128)S(1)}, f32[8,128]{1,0:T(8,128)S(1)}, bf16[32,128,128]{2,1,0:T(8,128)(2,1)}) custom-call(s32[1]{0:T(128)} %bitcast.x_ref, bf16[32,128,128]{2,1,0:T(8,128)(2,1)S(1)} %copy-done, f32[1,128]{1,0:T(1,128)S(1)} %bitcast.24, f32[1,128]{1,0:T(1,128)S(1)} %bitcast.31, ...), custom_call_target="tpu_custom_call" | custom-call | tf_op jit(solution)/shard_map/backward_blocks/pallas_call | solution.py:338
  28.3 0.0 collective-permute-done.2.rest_0_
  28.3 5.0 %backward_blocks.5 = (f32[128,1024]{1,0:T(8,128)S(1)}, f32[128,512]{1,0:T(8,128)S(1)}, f32[64,128]{1,0:T(8,128)S(1)}, f32[8,128]{1,0:T(8,128)S(1)}, bf16[32,128,128]{2,1,0:T(8,128)(2,1)}) custom-call(s32[1]{0:T(128)} %bitcast.x_ref, bf16[32,128,128]{2,1,0:T(8,128)(2,1)S(1)} %copy-done, f32[1,128]{1,0:T(1,128)S(1)} %bitcast.25, ...), custom_call_target="tpu_custom_call", output_to_operand_aliasing={{4}: (16, {})} | custom-call | tf_op jit(solution)/shard_map/backward_blocks/pallas_call | solution.py:338
  33.4 0.0 collective-permute-done.1.rest_0_
  33.4 5.1 %backward_blocks.6 = (f32[128,1024]{1,0:T(8,128)S(1)}, f32[128,512]{1,0:T(8,128)S(1)}, f32[64,128]{1,0:T(8,128)S(1)}, f32[8,128]{1,0:T(8,128)S(1)}, bf16[32,128,128]{2,1,0:T(8,128)(2,1)}) custom-call(s32[1]{0:T(128)} %bitcast.x_ref, bf16[32,128,128]{2,1,0:T(8,128)(2,1)S(1)} %copy-done, f32[1,128]{1,0:T(1,128)S(1)} %bitcast.26, ...), custom_call_target="tpu_custom_call", output_to_operand_aliasing={{4}: (16, {})} | custom-call | tf_op jit(solution)/shard_map/backward_blocks/pallas_call | solution.py:338
  38.5 0.0 collective-permute-done.rest_0_
  38.5 5.3 %backward_blocks.7 = (bf16[1664,128]{1,0:T(8,128)(2,1)S(1)}, bf16[32,128,128]{2,1,0:T(8,128)(2,1)}) custom-call(s32[1]{0:T(128)} %bitcast.x_ref, bf16[32,128,128]{2,1,0:T(8,128)(2,1)S(1)} %copy-done, f32[1,128]{1,0:T(1,128)S(1)} %bitcast.27, f32[1,128]{1,0:T(1,128)S(1)} %bitcast.34, ...), custom_call_target="tpu_custom_call", output_to_operand_aliasing={{1}: (16, {})} | custom-call | tf_op jit(solution)/shard_map/backward_blocks/pallas_call | solution.py:338
  43.7 39.8 %all_to_all.10 = bf16[16,104,128]{2,1,0:T(8,128)(2,1)S(1)} all-to-all(bf16[16,104,128]{2,1,0:T(8,128)(2,1)S(1)} %bitcast.20), channel_id=1, replica_groups=mesh['crop'=8,'z_lo'=4,'x'=4,'z_hi'=4] {'z_lo','x'}, dimensions={0} | all-to-all | bytes 851968 | tf_op jit(solution)/shard_map/all_to_all | solution.py:374
  83.5 0.1 reduce_sum.24
  83.6 18.2 %all-gather = bf16[416,128]{1,0:T(8,128)(2,1)S(1)} all-gather(bf16[104,128]{1,0:T(8,128)(2,1)S(1)} %reduce_sum.24), channel_id=2, replica_groups=mesh['crop'=8,'z_lo'=4,'x'=4,'z_hi'=4] {'z_hi'}, dimensions={0}, use_global_device_ids=true | all-gather | bytes 133120 | tf_op jit(solution)/shard_map/all_gather | solution.py:376
  101.9 0.1 broadcast_in_dim.19
  101.9 15.5 %all_to_all.11 = bf16[16,104,128]{2,1,0:T(8,128)(2,1)S(1)} all-to-all(bf16[16,104,128]{2,1,0:T(8,128)(2,1)S(1)} %broadcast_in_dim.19), channel_id=1, replica_groups=mesh['crop'=8,'z_lo'=4,'x'=4,'z_hi'=4] {'z_lo','x'}, dimensions={0} | all-to-all | bytes 851968 | tf_op jit(solution)/shard_map/all_to_all | solution.py:378
  117.4 1.0 unpack_sums.1
  (1 shorter events, 0.0 us)
Async XLA Ops:
  0.6 5.3 %copy-start = (bf16[32,128,128]{2,1,0:T(8,128)(2,1)S(1)}, bf16[32,128,128]{2,1,0:T(8,128)(2,1)}, u32[]{:S(2)}) copy-start(bf16[32,128,128]{2,1,0:T(8,128)(2,1)} %pair_ref.13) | copy-start | bytes 3145732
  0.7 5.3 %copy-start.1 = (bf16[128,512]{1,0:T(8,128)(2,1)S(1)}, bf16[128,512]{1,0:T(8,128)(2,1)}, u32[]{:S(2)}) copy-start(bf16[128,512]{1,0:T(8,128)(2,1)} %w_gate_ref.13) | copy-start | bytes 393220
  0.7 5.3 %copy-start.2 = (bf16[128,512]{1,0:T(8,128)(2,1)S(1)}, bf16[128,512]{1,0:T(8,128)(2,1)}, u32[]{:S(2)}) copy-start(bf16[128,512]{1,0:T(8,128)(2,1)} %w_up_ref.13) | copy-start | bytes 393220
  0.7 5.3 %copy-start.3 = (bf16[512,128]{1,0:T(8,128)(2,1)S(1)}, bf16[512,128]{1,0:T(8,128)(2,1)}, u32[]{:S(2)}) copy-start(bf16[512,128]{1,0:T(8,128)(2,1)} %w_down_ref.13) | copy-start | bytes 393220
  0.7 5.3 %copy-start.4 = (bf16[128,64]{0,1:T(8,128)(2,1)S(1)}, bf16[128,64]{0,1:T(8,128)(2,1)}, u32[]{:S(2)}) copy-start(bf16[128,64]{0,1:T(8,128)(2,1)} %param.16) | copy-start | bytes 49156
  0.7 5.3 %copy-start.5 = (s32[32,128]{1,0:T(8,128)S(1)}, s32[32,128]{1,0:T(8,128)}, u32[]{:S(2)}) copy-start(s32[32,128]{1,0:T(8,128)} %targets_ref.13) | copy-start | bytes 49156
  0.7 5.3 %copy-start.6 = (s32[32,128]{1,0:T(8,128)S(1)}, s32[32,128]{1,0:T(8,128)}, u32[]{:S(2)}) copy-start(s32[32,128]{1,0:T(8,128)} %mask_ref.13) | copy-start | bytes 49156
  0.7 5.3 %copy-start.7 = (f32[128]{0:T(128)S(1)}, f32[128]{0:T(128)}, u32[]{:S(2)}) copy-start(f32[128]{0:T(128)} %param.11) | copy-start | bytes 1540
  0.7 5.3 %copy-start.8 = (f32[128]{0:T(128)S(1)}, f32[128]{0:T(128)}, u32[]{:S(2)}) copy-start(f32[128]{0:T(128)} %param.12) | copy-start | bytes 1540
  0.7 5.3 %copy-start.9 = (f32[64]{0:T(128)S(1)}, f32[64]{0:T(128)}, u32[]{:S(2)}) copy-start(f32[64]{0:T(128)} %param.17) | copy-start | bytes 772
  4.4 19.1 %collective-permute-start.3 = (bf16[528,128]{1,0:T(8,128)(2,1)}, bf16[528,128]{1,0:T(8,128)(2,1)S(1)}, u32[]{:S(2)}, u32[]{:S(2)}) collective-permute-start(bf16[528,128]{1,0:T(8,128)(2,1)} %forward_send.3), channel_id=1, source_target_pairs={{0,0},{1,16},{2,32},{3,48},{4,4},{5,20},{6,36},{7,52},{8,8},{9,24}... | collective-permute-start | bytes 405512 | tf_op jit(solution)/shard_map/ppermute | solution.py:319
  7.9 20.4 %collective-permute-start.2 = (bf16[528,128]{1,0:T(8,128)(2,1)S(1)}, bf16[528,128]{1,0:T(8,128)(2,1)S(1)}, u32[]{:S(2)}, u32[]{:S(2)}) collective-permute-start(bf16[528,128]{1,0:T(8,128)(2,1)S(1)} %forward_send.4), channel_id=1, source_target_pairs={{0,4},{1,20},{2,36},{3,52},{4,8},{5,24},{6,40},{7,56},{8,12},{9,28... | collective-permute-start | bytes 405512 | tf_op jit(solution)/shard_map/ppermute | solution.py:319
  15.3 18.1 %collective-permute-start.1 = (bf16[528,128]{1,0:T(8,128)(2,1)S(1)}, bf16[528,128]{1,0:T(8,128)(2,1)S(1)}, u32[]{:S(2)}, u32[]{:S(2)}) collective-permute-start(bf16[528,128]{1,0:T(8,128)(2,1)S(1)} %get-tuple-element.39), channel_id=1, source_target_pairs={{0,8},{1,24},{2,40},{3,56},{4,12},{5,28},{6,44},{7,60},{8,0},{9,16... | collective-permute-start | bytes 405512 | tf_op jit(solution)/shard_map/ppermute | solution.py:319
  20.0 18.5 %collective-permute-start = (bf16[528,128]{1,0:T(8,128)(2,1)S(1)}, bf16[528,128]{1,0:T(8,128)(2,1)S(1)}, u32[]{:S(2)}, u32[]{:S(2)}) collective-permute-start(bf16[528,128]{1,0:T(8,128)(2,1)S(1)} %get-tuple-element.38), channel_id=1, source_target_pairs={{0,12},{1,28},{2,44},{3,60},{4,0},{5,16},{6,32},{7,48},{8,4},{9,20... | collective-permute-start | bytes 405512 | tf_op jit(solution)/shard_map/ppermute | solution.py:319

commit v5 on v4

--- a/solution.py
+++ b/solution.py
@@ -19,7 +19,7 @@
 ROWS = SUB // SIDE
 WIRE = PAIRS // 2 + 16
 GROUP = 16
-SHARE = 104
+SHARE = 88
 PACK = GROUP * SHARE
 SENDS = ((0, 1), (1, 1), (2, 2))
 BACKS = ((0, 1), (1, 1), (2, 1), (3, 1))
@@ -114,7 +114,7 @@
         acc_outs, rest = rest[:4], rest[4:]
     grad_ref, *rest = rest
     (acc_gu, acc_down, acc_head, acc_small, w_gu_ref, normed_s, xhat_s, rstd_s, gate_up_s, hidden_s,
-     updated_s, grad_s, gu_grad_s, codes_s, half_grad_s, grad_t_s, wire_s, sems) = rest
+     updated_s, grad_s, gu_grad_s, codes_s, half_grad_s, wire_s, sems) = rest
     accs = (acc_gu, acc_down, acc_head, acc_small)
     moves = [(wire_ref, wire_s.at[n]) for n, wire_ref in enumerate(wire_refs)]
     if not first:
@@ -187,8 +187,6 @@
     half_grad_s[...] = half_grad
     head_bias_sum = jnp.sum(half_grad.astype(F32), axis=1, keepdims=True)
     grad_s[...] = dot(half_grad, head_t_ref[...], 0, 0)
-    grad_t = dot(head_t_ref[...], half_grad, 0, 0).astype(BF16)
-    grad_t_s[...] = grad_t
 
     def backward(n, carry):
         gain_sum, bias_sum = carry
@@ -220,7 +218,7 @@
         0, STEPS, backward, (jnp.zeros((1, C), F32), jnp.zeros((1, C), F32))
     )
     head_sum = jnp.dot(half_grad_s[...], updated_s[...], preferred_element_type=F32)
-    down_sum = jnp.dot(grad_t_s[...], hidden_s[...], preferred_element_type=F32)
+    down_sum = jnp.dot(half_grad_s[...], hidden_s[...], preferred_element_type=F32)
     gu_sum = dot(normed_s[...], gu_grad_s[...], 0, 0)
     head_bias_row = jnp.concatenate(
         [jnp.broadcast_to(head_bias_sum, (NB, 128)), jnp.zeros((NB, 128), F32)], axis=0
@@ -245,23 +243,32 @@
             for b in range(8):
                 pack_ref[pl.ds(b * 128, 128), :] = acc_gu[:, b * 128 : b * 128 + 128].astype(BF16)
             for b in range(4):
-                pack_ref[pl.ds(1024 + b * 128, 128), :] = acc_down[
+                pack_ref[pl.ds(1024 + b * NB, NB), :] = acc_down[
                     :, b * 128 : b * 128 + 128
                 ].astype(BF16)
-            pack_ref[pl.ds(1536, NB), :] = acc_head[...].astype(BF16)
-            tail = jnp.concatenate([acc_small[...], jnp.zeros((PACK - 1608, 128), F32)], axis=0)
-            pack_ref[pl.ds(1600, PACK - 1600), :] = tail.astype(BF16)
-
-
-def unpack_kernel(scale, pack_ref, gain_ref, bias_ref, gate_ref, up_ref, down_ref, head_ref, head_bias_ref):
+            pack_ref[pl.ds(1280, NB), :] = acc_head[...].astype(BF16)
+            tail = jnp.concatenate([acc_small[...], jnp.zeros((PACK - 1352, 128), F32)], axis=0)
+            pack_ref[pl.ds(1344, PACK - 1344), :] = tail.astype(BF16)
+
+
+def unpack_kernel(
+    scale, pack_ref, head_t_ref, gain_ref, bias_ref, gate_ref, up_ref, down_ref, head_ref,
+    head_bias_ref,
+):
     def block(b):
         return pack_ref[pl.ds(b * 128, 128), :].astype(F32) * scale
 
+    head_t = head_t_ref[...].astype(F32)
+    head_t = head_t - jnp.mean(head_t, axis=0, keepdims=True)
+    head_high = head_t.astype(BF16)
+    head_low = (head_t - head_high.astype(F32)).astype(BF16)
     for b in range(4):
         gate_ref[:, b * 128 : b * 128 + 128] = block(b)
         up_ref[:, b * 128 : b * 128 + 128] = block(4 + b)
-        down_ref[pl.ds(b * 128, 128), :] = block(8 + b).T
-    tail = block(12)
+        by_bin = pack_ref[pl.ds(1024 + b * NB, NB), :]
+        down = dot(by_bin, head_high, 0, 0) + dot(by_bin, head_low, 0, 0)
+        down_ref[pl.ds(b * 128, 128), :] = down * scale
+    tail = pack_ref[pl.ds(1280, 128), :].astype(F32) * scale
     head_ref[...] = tail[:NB]
     gain_ref[...] = tail[NB : NB + 1]
     bias_ref[...] = tail[NB + 1 : NB + 2]
@@ -325,7 +332,7 @@
         wires += arrived
     sums = [
         jax.ShapeDtypeStruct((C, 2 * FF), F32),
-        jax.ShapeDtypeStruct((C, FF), F32),
+        jax.ShapeDtypeStruct((NB, FF), F32),
         jax.ShapeDtypeStruct((NB, C), F32),
         jax.ShapeDtypeStruct((8, C), F32),
     ]
@@ -357,7 +364,6 @@
                     pltpu.VMEM((PAIRS, 2 * FF), BF16),
                     pltpu.VMEM((2 * SIDE, 128), F32),
                     pltpu.VMEM((NB, PAIRS), BF16),
-                    pltpu.VMEM((C, PAIRS), BF16),
                     pltpu.VMEM((count, WIRE, 128), BF16),
                     pltpu.SemaphoreType.DMA((count if first else count + 4,)),
                 ],
@@ -392,7 +398,7 @@
         ],
         compiler_params=params,
         name="unpack_sums",
-    )(pack)
+    )(pack, head_weight.T)
     gain_tot, bias_tot, gate_tot, up_tot, down_tot, head_tot, head_bias_tot = outs
     return (
         pair_grad, gain_tot[0], bias_tot[0], gate_tot, up_tot, down_tot, head_tot.T,

time: 119 us -> 117 us (0.983)
  the two profiles are of different devices: /device:TPU:8 before, /device:TPU:16 now
where the time goes in v5:
time: 117 us; the launch traced here: 116 us
  blocking collectives  71.2 us (61%)
  Pallas kernels  31 us (26%)
  starting transfers between devices  13.1 us (11%)
    all_to_all x1, blocking collectives, on_device(): lax.all_to_all(pack.reshape(GROUP, SHARE, 128), ('z_lo', 'x'), 0, 0)  38.5 us
    pallas_call x4, Pallas kernels, on_device(): pl.pallas_call(functools.partial(back_kernel, shift, count), grid_spec=pl...  20.4 us
    all_gather x1, blocking collectives, on_device(): shares = lax.all_gather(share, 'z_hi')  18.2 us
    all_to_all x1, blocking collectives, on_device(): lax.all_to_all(jnp.broadcast_to(share, (GROUP, SHARE, 128)), ('z_lo', 'x'...  14.5 us
    ppermute x4, starting transfers between devices, send(): lax.ppermute(wire, GRID_AXES, route)  13.1 us
    pallas_call x3, Pallas kernels, send(): pl.pallas_call(functools.partial(send_kernel, shift), grid_spec=pltpu.Pre...  9.53 us
  transfers between devices with their start and end apart: 4, of which 0 were waited for; matrix products, arithmetic and copies ran while one was open for 0% of the time, Pallas kernels for 18%

profile of v5, /device:TPU:16, one launch (start us, length us, event | category | flops | bytes accessed | tf_op | source)
XLA Modules:
  0.0 116.4 jit_solution(12902778564457392005)
XLA Ops:
  0.6 0.0 copy-start
  0.7 0.0 copy-start.1
  0.7 0.0 copy-start.2
  0.7 0.0 copy-start.3
  0.7 0.0 copy-start.4
  0.7 0.0 copy-start.5
  0.7 0.0 copy-start.6
  0.7 0.0 copy-start.7
  0.7 0.0 copy-start.8
  0.7 0.0 copy-start.9
  0.7 3.7 %forward_send.3 = bf16[528,128]{1,0:T(8,128)(2,1)} custom-call(s32[1]{0:T(128)} %bitcast.x_ref, bf16[32,128,128]{2,1,0:T(8,128)(2,1)} %pair_ref.13, f32[1,128]{1,0:T(1,128)} %bitcast.22, f32[1,128]{1,0:T(1,128)} %bitcast.29, bf16[128,512]{1,0:T(8,128)(2,1)} %w_gate_ref.13, bf16[128,512]{1,0:T(8,128)(2,1)} %w_up_ref.13, bf16[512,128]{1,0:T(8,128)(2,1)} %w_down_ref.13, ...), custom_call_target="tpu_custom_call" | custom-call | tf_op jit(solution)/shard_map/forward_send/pallas_call | solution.py:300
  4.4 1.6 %collective-permute-start.3 = (bf16[528,128]{1,0:T(8,128)(2,1)}, bf16[528,128]{1,0:T(8,128)(2,1)S(1)}, u32[]{:S(2)}, u32[]{:S(2)}) collective-permute-start(bf16[528,128]{1,0:T(8,128)(2,1)} %forward_send.3), channel_id=1, source_target_pairs={{0,0},{1,16},{2,32},{3,48},{4,4},{5,20},{6,36},{7,52},{8,8},{9,24}... | collective-permute-start | bytes 405512 | tf_op jit(solution)/shard_map/ppermute | solution.py:326
  6.0 0.0 copy-done
  6.0 0.0 copy-done.1
  6.0 0.0 copy-done.2
  6.0 0.0 copy-done.3
  6.0 0.0 copy-done.4
  6.0 0.0 copy-done.5
  6.0 0.0 copy-done.6
  6.0 0.0 copy-done.7
  6.0 0.0 copy-done.8
  6.0 0.0 copy-done.9
  6.0 1.8 %forward_send.4 = bf16[528,128]{1,0:T(8,128)(2,1)S(1)} custom-call(s32[1]{0:T(128)} %bitcast.x_ref, bf16[32,128,128]{2,1,0:T(8,128)(2,1)S(1)} %copy-done, f32[1,128]{1,0:T(1,128)S(1)} %bitcast.23, f32[1,128]{1,0:T(1,128)S(1)} %bitcast.30, bf16[128,512]{1,0:T(8,128)(2,1)S(1)} %copy-done.1, bf16[128,512]{1,0:T(8,128)(2,1)S(1)} %copy-done.2, ...), custom_call_target="tpu_custom_call" | custom-call | tf_op jit(solution)/shard_map/forward_send/pallas_call | solution.py:300
  7.9 3.4 %collective-permute-start.2 = (bf16[528,128]{1,0:T(8,128)(2,1)S(1)}, bf16[528,128]{1,0:T(8,128)(2,1)S(1)}, u32[]{:S(2)}, u32[]{:S(2)}) collective-permute-start(bf16[528,128]{1,0:T(8,128)(2,1)S(1)} %forward_send.4), channel_id=1, source_target_pairs={{0,4},{1,20},{2,36},{3,52},{4,8},{5,24},{6,40},{7,56},{8,12},{9,28... | collective-permute-start | bytes 405512 | tf_op jit(solution)/shard_map/ppermute | solution.py:326
  11.3 4.0 %forward_send.5 = (bf16[528,128]{1,0:T(8,128)(2,1)S(1)}, bf16[528,128]{1,0:T(8,128)(2,1)S(1)}) custom-call(s32[1]{0:T(128)} %bitcast.x_ref, bf16[32,128,128]{2,1,0:T(8,128)(2,1)S(1)} %copy-done, f32[1,128]{1,0:T(1,128)S(1)} %bitcast.24, f32[1,128]{1,0:T(1,128)S(1)} %bitcast.31, bf16[128,512]{1,0:T(8,128)(2,1)S(1)} %copy-done.1, ...), custom_call_target="tpu_custom_call" | custom-call | tf_op jit(solution)/shard_map/forward_send/pallas_call | solution.py:300
  15.3 4.6 %collective-permute-start.1 = (bf16[528,128]{1,0:T(8,128)(2,1)S(1)}, bf16[528,128]{1,0:T(8,128)(2,1)S(1)}, u32[]{:S(2)}, u32[]{:S(2)}) collective-permute-start(bf16[528,128]{1,0:T(8,128)(2,1)S(1)} %get-tuple-element.39), channel_id=1, source_target_pairs={{0,8},{1,24},{2,40},{3,56},{4,12},{5,28},{6,44},{7,60},{8,0},{9,16... | collective-permute-start | bytes 405512 | tf_op jit(solution)/shard_map/ppermute | solution.py:326
  20.0 3.5 %collective-permute-start = (bf16[528,128]{1,0:T(8,128)(2,1)S(1)}, bf16[528,128]{1,0:T(8,128)(2,1)S(1)}, u32[]{:S(2)}, u32[]{:S(2)}) collective-permute-start(bf16[528,128]{1,0:T(8,128)(2,1)S(1)} %get-tuple-element.38), channel_id=1, source_target_pairs={{0,12},{1,28},{2,44},{3,60},{4,0},{5,16},{6,32},{7,48},{8,4},{9,20... | collective-permute-start | bytes 405512 | tf_op jit(solution)/shard_map/ppermute | solution.py:326
  23.5 0.0 collective-permute-done.3.rest_0_
  23.5 4.8 %backward_blocks.4 = (f32[128,1024]{1,0:T(8,128)S(1)}, f32[64,512]{1,0:T(8,128)S(1)}, f32[64,128]{1,0:T(8,128)S(1)}, f32[8,128]{1,0:T(8,128)S(1)}, bf16[32,128,128]{2,1,0:T(8,128)(2,1)}) custom-call(s32[1]{0:T(128)} %bitcast.x_ref, bf16[32,128,128]{2,1,0:T(8,128)(2,1)S(1)} %copy-done, f32[1,128]{1,0:T(1,128)S(1)} %bitcast.25, f32[1,128]{1,0:T(1,128)S(1)} %bitcast.32, ...), custom_call_target="tpu_custom_call" | custom-call | tf_op jit(solution)/shard_map/backward_blocks/pallas_call | solution.py:345
  28.3 0.0 collective-permute-done.2.rest_0_
  28.3 5.2 %backward_blocks.5 = (f32[128,1024]{1,0:T(8,128)S(1)}, f32[64,512]{1,0:T(8,128)S(1)}, f32[64,128]{1,0:T(8,128)S(1)}, f32[8,128]{1,0:T(8,128)S(1)}, bf16[32,128,128]{2,1,0:T(8,128)(2,1)}) custom-call(s32[1]{0:T(128)} %bitcast.x_ref, bf16[32,128,128]{2,1,0:T(8,128)(2,1)S(1)} %copy-done, f32[1,128]{1,0:T(1,128)S(1)} %bitcast.26, ...), custom_call_target="tpu_custom_call", output_to_operand_aliasing={{4}: (16, {})} | custom-call | tf_op jit(solution)/shard_map/backward_blocks/pallas_call | solution.py:345
  33.5 0.0 collective-permute-done.1.rest_0_
  33.5 5.2 %backward_blocks.6 = (f32[128,1024]{1,0:T(8,128)S(1)}, f32[64,512]{1,0:T(8,128)S(1)}, f32[64,128]{1,0:T(8,128)S(1)}, f32[8,128]{1,0:T(8,128)S(1)}, bf16[32,128,128]{2,1,0:T(8,128)(2,1)}) custom-call(s32[1]{0:T(128)} %bitcast.x_ref, bf16[32,128,128]{2,1,0:T(8,128)(2,1)S(1)} %copy-done, f32[1,128]{1,0:T(1,128)S(1)} %bitcast.27, ...), custom_call_target="tpu_custom_call", output_to_operand_aliasing={{4}: (16, {})} | custom-call | tf_op jit(solution)/shard_map/backward_blocks/pallas_call | solution.py:345
  38.6 0.0 collective-permute-done.rest_0_
  38.6 5.4 %backward_blocks.7 = (bf16[1408,128]{1,0:T(8,128)(2,1)S(1)}, bf16[32,128,128]{2,1,0:T(8,128)(2,1)}) custom-call(s32[1]{0:T(128)} %bitcast.x_ref, bf16[32,128,128]{2,1,0:T(8,128)(2,1)S(1)} %copy-done, f32[1,128]{1,0:T(1,128)S(1)} %bitcast.28, f32[1,128]{1,0:T(1,128)S(1)} %bitcast.35, ...), custom_call_target="tpu_custom_call", output_to_operand_aliasing={{1}: (16, {})} | custom-call | tf_op jit(solution)/shard_map/backward_blocks/pallas_call | solution.py:345
  44.0 38.5 %all_to_all.10 = bf16[16,88,128]{2,1,0:T(8,128)(2,1)S(1)} all-to-all(bf16[16,88,128]{2,1,0:T(8,128)(2,1)S(1)} %bitcast.21), channel_id=1, replica_groups=mesh['crop'=8,'z_lo'=4,'x'=4,'z_hi'=4] {'z_lo','x'}, dimensions={0} | all-to-all | bytes 720896 | tf_op jit(solution)/shard_map/all_to_all | solution.py:380
  82.5 0.1 reduce_sum.24
  82.6 18.2 %all-gather = bf16[352,128]{1,0:T(8,128)(2,1)S(1)} all-gather(bf16[88,128]{1,0:T(8,128)(2,1)S(1)} %reduce_sum.24), channel_id=2, replica_groups=mesh['crop'=8,'z_lo'=4,'x'=4,'z_hi'=4] {'z_hi'}, dimensions={0}, use_global_device_ids=true | all-gather | bytes 112640 | tf_op jit(solution)/shard_map/all_gather | solution.py:382
  100.8 14.5 %all_to_all.11 = bf16[16,88,128]{2,1,0:T(8,128)(2,1)S(1)} all-to-all(bf16[16,88,128]{2,1,0:T(8,128)(2,1)S(1)} %broadcast_in_dim.19), channel_id=1, replica_groups=mesh['crop'=8,'z_lo'=4,'x'=4,'z_hi'=4] {'z_lo','x'}, dimensions={0} | all-to-all | bytes 720896 | tf_op jit(solution)/shard_map/all_to_all | solution.py:384
  115.3 1.0 unpack_sums.1
  (2 shorter events, 0.1 us)
Async XLA Ops:
  0.6 5.3 %copy-start = (bf16[32,128,128]{2,1,0:T(8,128)(2,1)S(1)}, bf16[32,128,128]{2,1,0:T(8,128)(2,1)}, u32[]{:S(2)}) copy-start(bf16[32,128,128]{2,1,0:T(8,128)(2,1)} %pair_ref.13) | copy-start | bytes 3145732
  0.7 5.3 %copy-start.1 = (bf16[128,512]{1,0:T(8,128)(2,1)S(1)}, bf16[128,512]{1,0:T(8,128)(2,1)}, u32[]{:S(2)}) copy-start(bf16[128,512]{1,0:T(8,128)(2,1)} %w_gate_ref.13) | copy-start | bytes 393220
  0.7 5.3 %copy-start.2 = (bf16[128,512]{1,0:T(8,128)(2,1)S(1)}, bf16[128,512]{1,0:T(8,128)(2,1)}, u32[]{:S(2)}) copy-start(bf16[128,512]{1,0:T(8,128)(2,1)} %w_up_ref.13) | copy-start | bytes 393220
  0.7 5.3 %copy-start.3 = (bf16[512,128]{1,0:T(8,128)(2,1)S(1)}, bf16[512,128]{1,0:T(8,128)(2,1)}, u32[]{:S(2)}) copy-start(bf16[512,128]{1,0:T(8,128)(2,1)} %w_down_ref.13) | copy-start | bytes 393220
  0.7 5.3 %copy-start.4 = (bf16[128,64]{0,1:T(8,128)(2,1)S(1)}, bf16[128,64]{0,1:T(8,128)(2,1)}, u32[]{:S(2)}) copy-start(bf16[128,64]{0,1:T(8,128)(2,1)} %param.16) | copy-start | bytes 49156
  0.7 5.3 %copy-start.5 = (s32[32,128]{1,0:T(8,128)S(1)}, s32[32,128]{1,0:T(8,128)}, u32[]{:S(2)}) copy-start(s32[32,128]{1,0:T(8,128)} %targets_ref.13) | copy-start | bytes 49156
  0.7 5.3 %copy-start.6 = (s32[32,128]{1,0:T(8,128)S(1)}, s32[32,128]{1,0:T(8,128)}, u32[]{:S(2)}) copy-start(s32[32,128]{1,0:T(8,128)} %mask_ref.13) | copy-start | bytes 49156
  0.7 5.3 %copy-start.7 = (f32[128]{0:T(128)S(1)}, f32[128]{0:T(128)}, u32[]{:S(2)}) copy-start(f32[128]{0:T(128)} %param.11) | copy-start | bytes 1540
  0.7 5.3 %copy-start.8 = (f32[128]{0:T(128)S(1)}, f32[128]{0:T(128)}, u32[]{:S(2)}) copy-start(f32[128]{0:T(128)} %param.12) | copy-start | bytes 1540
  0.7 5.3 %copy-start.9 = (f32[64]{0:T(128)S(1)}, f32[64]{0:T(128)}, u32[]{:S(2)}) copy-start(f32[64]{0:T(128)} %param.17) | copy-start | bytes 772
  4.4 19.1 %collective-permute-start.3 = (bf16[528,128]{1,0:T(8,128)(2,1)}, bf16[528,128]{1,0:T(8,128)(2,1)S(1)}, u32[]{:S(2)}, u32[]{:S(2)}) collective-permute-start(bf16[528,128]{1,0:T(8,128)(2,1)} %forward_send.3), channel_id=1, source_target_pairs={{0,0},{1,16},{2,32},{3,48},{4,4},{5,20},{6,36},{7,52},{8,8},{9,24}... | collective-permute-start | bytes 405512 | tf_op jit(solution)/shard_map/ppermute | solution.py:326
  7.9 20.4 %collective-permute-start.2 = (bf16[528,128]{1,0:T(8,128)(2,1)S(1)}, bf16[528,128]{1,0:T(8,128)(2,1)S(1)}, u32[]{:S(2)}, u32[]{:S(2)}) collective-permute-start(bf16[528,128]{1,0:T(8,128)(2,1)S(1)} %forward_send.4), channel_id=1, source_target_pairs={{0,4},{1,20},{2,36},{3,52},{4,8},{5,24},{6,40},{7,56},{8,12},{9,28... | collective-permute-start | bytes 405512 | tf_op jit(solution)/shard_map/ppermute | solution.py:326
  15.3 18.1 %collective-permute-start.1 = (bf16[528,128]{1,0:T(8,128)(2,1)S(1)}, bf16[528,128]{1,0:T(8,128)(2,1)S(1)}, u32[]{:S(2)}, u32[]{:S(2)}) collective-permute-start(bf16[528,128]{1,0:T(8,128)(2,1)S(1)} %get-tuple-element.39), channel_id=1, source_target_pairs={{0,8},{1,24},{2,40},{3,56},{4,12},{5,28},{6,44},{7,60},{8,0},{9,16... | collective-permute-start | bytes 405512 | tf_op jit(solution)/shard_map/ppermute | solution.py:326
  20.0 18.7 %collective-permute-start = (bf16[528,128]{1,0:T(8,128)(2,1)S(1)}, bf16[528,128]{1,0:T(8,128)(2,1)S(1)}, u32[]{:S(2)}, u32[]{:S(2)}) collective-permute-start(bf16[528,128]{1,0:T(8,128)(2,1)S(1)} %get-tuple-element.38), channel_id=1, source_target_pairs={{0,12},{1,28},{2,44},{3,60},{4,0},{5,16},{6,32},{7,48},{8,4},{9,20... | collective-permute-start | bytes 405512 | tf_op jit(solution)/shard_map/ppermute | solution.py:326

commit v6 on v5

--- a/solution.py
+++ b/solution.py
@@ -21,7 +21,7 @@
 GROUP = 16
 SHARE = 88
 PACK = GROUP * SHARE
-SENDS = ((0, 1), (1, 1), (2, 2))
+SENDS = ((0, 1), (1, 1), (2, 1), (3, 1))
 BACKS = ((0, 1), (1, 1), (2, 1), (3, 1))
 GRID_AXES = ("z_lo", "x", "z_hi")
 VMEM_ALONE = 60 * 1024 * 1024
@@ -167,7 +167,7 @@
     symmetric = half + jnp.concatenate([mirror[:NB], mirror[NB:]], axis=1)
     symmetric = symmetric - jnp.max(symmetric, axis=0, keepdims=True)
     exped = jnp.exp(symmetric)
-    prob = exped / jnp.sum(exped, axis=0, keepdims=True)
+    prob = exped * (1.0 / jnp.sum(exped, axis=0, keepdims=True))
     lane_shift = lax.rem(128 - lax.rem(x_ref[0] + 4 - shift - turn, 4) * SIDE, 128)
     codes_s[pl.ds(0, SIDE), :] = targets_ref[...].astype(F32)
     codes_s[pl.ds(SIDE, SIDE), :] = mask_ref[...].astype(F32)

time: 117 us -> 116 us (level)
  the two profiles are of different devices: /device:TPU:16 before, /device:TPU:8 now
where the time goes in v6:
time: 116 us
  blocking collectives  71.3 us (61%)
  Pallas kernels  30.6 us (26%)
  starting transfers between devices  13.1 us (11%)
    all_to_all x1, blocking collectives, on_device(): lax.all_to_all(pack.reshape(GROUP, SHARE, 128), ('z_lo', 'x'), 0, 0)  36.8 us
    pallas_call x4, Pallas kernels, on_device(): pl.pallas_call(functools.partial(back_kernel, shift, count), grid_spec=pl...  20.4 us
    all_gather x1, blocking collectives, on_device(): shares = lax.all_gather(share, 'z_hi')  19.7 us
    all_to_all x1, blocking collectives, on_device(): lax.all_to_all(jnp.broadcast_to(share, (GROUP, SHARE, 128)), ('z_lo', 'x'...  14.7 us
    ppermute x4, starting transfers between devices, send(): lax.ppermute(wire, GRID_AXES, route)  13.1 us
    pallas_call x4, Pallas kernels, send(): pl.pallas_call(functools.partial(send_kernel, shift), grid_spec=pltpu.Pre...  9.16 us
  transfers between devices with their start and end apart: 4, of which 0 were waited for; matrix products, arithmetic and copies ran while one was open for 0% of the time, Pallas kernels for 18%

profile of v6, /device:TPU:8, one launch (start us, length us, event | category | flops | bytes accessed | tf_op | source)
XLA Modules:
  0.0 116.1 jit_solution(9488589861761512693)
XLA Ops:
  0.6 0.0 copy-start
  0.7 0.0 copy-start.1
  0.7 0.0 copy-start.2
  0.7 0.0 copy-start.3
  0.7 0.0 copy-start.4
  0.7 0.0 copy-start.5
  0.7 0.0 copy-start.6
  0.7 0.0 copy-start.7
  0.7 0.0 copy-start.8
  0.7 0.0 copy-start.9
  0.7 3.7 %forward_send.4 = bf16[528,128]{1,0:T(8,128)(2,1)} custom-call(s32[1]{0:T(128)} %bitcast.x_ref, bf16[32,128,128]{2,1,0:T(8,128)(2,1)} %pair_ref.15, f32[1,128]{1,0:T(1,128)} %bitcast.23, f32[1,128]{1,0:T(1,128)} %bitcast.31, bf16[128,512]{1,0:T(8,128)(2,1)} %w_gate_ref.15, bf16[128,512]{1,0:T(8,128)(2,1)} %w_up_ref.15, bf16[512,128]{1,0:T(8,128)(2,1)} %w_down_ref.15, ...), custom_call_target="tpu_custom_call" | custom-call | tf_op jit(solution)/shard_map/forward_send/pallas_call | solution.py:300
  4.4 1.6 %collective-permute-start.3 = (bf16[528,128]{1,0:T(8,128)(2,1)}, bf16[528,128]{1,0:T(8,128)(2,1)S(1)}, u32[]{:S(2)}, u32[]{:S(2)}) collective-permute-start(bf16[528,128]{1,0:T(8,128)(2,1)} %forward_send.4), channel_id=1, source_target_pairs={{0,0},{1,16},{2,32},{3,48},{4,4},{5,20},{6,36},{7,52},{8,8},{9,24}... | collective-permute-start | bytes 405512 | tf_op jit(solution)/shard_map/ppermute | solution.py:326
  6.0 0.0 copy-done
  6.0 0.0 copy-done.1
  6.0 0.0 copy-done.2
  6.0 0.0 copy-done.3
  6.0 0.0 copy-done.4
  6.0 0.0 copy-done.5
  6.0 0.0 copy-done.6
  6.0 0.0 copy-done.7
  6.0 0.0 copy-done.8
  6.0 0.0 copy-done.9
  6.0 1.8 %forward_send.5 = bf16[528,128]{1,0:T(8,128)(2,1)S(1)} custom-call(s32[1]{0:T(128)} %bitcast.x_ref, bf16[32,128,128]{2,1,0:T(8,128)(2,1)S(1)} %copy-done, f32[1,128]{1,0:T(1,128)S(1)} %bitcast.24, f32[1,128]{1,0:T(1,128)S(1)} %bitcast.32, bf16[128,512]{1,0:T(8,128)(2,1)S(1)} %copy-done.1, bf16[128,512]{1,0:T(8,128)(2,1)S(1)} %copy-done.2, ...), custom_call_target="tpu_custom_call" | custom-call | tf_op jit(solution)/shard_map/forward_send/pallas_call | solution.py:300
  7.9 3.4 %collective-permute-start.2 = (bf16[528,128]{1,0:T(8,128)(2,1)S(1)}, bf16[528,128]{1,0:T(8,128)(2,1)S(1)}, u32[]{:S(2)}, u32[]{:S(2)}) collective-permute-start(bf16[528,128]{1,0:T(8,128)(2,1)S(1)} %forward_send.5), channel_id=1, source_target_pairs={{0,4},{1,20},{2,36},{3,52},{4,8},{5,24},{6,40},{7,56},{8,12},{9,28... | collective-permute-start | bytes 405512 | tf_op jit(solution)/shard_map/ppermute | solution.py:326
  11.3 1.8 %forward_send.6 = bf16[528,128]{1,0:T(8,128)(2,1)S(1)} custom-call(s32[1]{0:T(128)} %bitcast.x_ref, bf16[32,128,128]{2,1,0:T(8,128)(2,1)S(1)} %copy-done, f32[1,128]{1,0:T(1,128)S(1)} %bitcast.25, f32[1,128]{1,0:T(1,128)S(1)} %bitcast.33, bf16[128,512]{1,0:T(8,128)(2,1)S(1)} %copy-done.1, bf16[128,512]{1,0:T(8,128)(2,1)S(1)} %copy-done.2, ...), custom_call_target="tpu_custom_call" | custom-call | tf_op jit(solution)/shard_map/forward_send/pallas_call | solution.py:300
  13.1 4.7 %collective-permute-start.1 = (bf16[528,128]{1,0:T(8,128)(2,1)S(1)}, bf16[528,128]{1,0:T(8,128)(2,1)S(1)}, u32[]{:S(2)}, u32[]{:S(2)}) collective-permute-start(bf16[528,128]{1,0:T(8,128)(2,1)S(1)} %forward_send.6), channel_id=1, source_target_pairs={{0,8},{1,24},{2,40},{3,56},{4,12},{5,28},{6,44},{7,60},{8,0},{9,16... | collective-permute-start | bytes 405512 | tf_op jit(solution)/shard_map/ppermute | solution.py:326
  17.8 1.8 %forward_send.7 = bf16[528,128]{1,0:T(8,128)(2,1)S(1)} custom-call(s32[1]{0:T(128)} %bitcast.x_ref, bf16[32,128,128]{2,1,0:T(8,128)(2,1)S(1)} %copy-done, f32[1,128]{1,0:T(1,128)S(1)} %bitcast.26, f32[1,128]{1,0:T(1,128)S(1)} %bitcast.34, bf16[128,512]{1,0:T(8,128)(2,1)S(1)} %copy-done.1, bf16[128,512]{1,0:T(8,128)(2,1)S(1)} %copy-done.2, ...), custom_call_target="tpu_custom_call" | custom-call | tf_op jit(solution)/shard_map/forward_send/pallas_call | solution.py:300
  19.6 3.5 %collective-permute-start = (bf16[528,128]{1,0:T(8,128)(2,1)S(1)}, bf16[528,128]{1,0:T(8,128)(2,1)S(1)}, u32[]{:S(2)}, u32[]{:S(2)}) collective-permute-start(bf16[528,128]{1,0:T(8,128)(2,1)S(1)} %forward_send.7), channel_id=1, source_target_pairs={{0,12},{1,28},{2,44},{3,60},{4,0},{5,16},{6,32},{7,48},{8,4},{9,20... | collective-permute-start | bytes 405512 | tf_op jit(solution)/shard_map/ppermute | solution.py:326
  23.2 0.0 collective-permute-done.3.rest_0_
  23.2 4.8 %backward_blocks.4 = (f32[128,1024]{1,0:T(8,128)S(1)}, f32[64,512]{1,0:T(8,128)S(1)}, f32[64,128]{1,0:T(8,128)S(1)}, f32[8,128]{1,0:T(8,128)S(1)}, bf16[32,128,128]{2,1,0:T(8,128)(2,1)}) custom-call(s32[1]{0:T(128)} %bitcast.x_ref, bf16[32,128,128]{2,1,0:T(8,128)(2,1)S(1)} %copy-done, f32[1,128]{1,0:T(1,128)S(1)} %bitcast.27, f32[1,128]{1,0:T(1,128)S(1)} %bitcast.35, ...), custom_call_target="tpu_custom_call" | custom-call | tf_op jit(solution)/shard_map/backward_blocks/pallas_call | solution.py:345
  27.9 0.0 collective-permute-done.2.rest_0_
  27.9 5.2 %backward_blocks.5 = (f32[128,1024]{1,0:T(8,128)S(1)}, f32[64,512]{1,0:T(8,128)S(1)}, f32[64,128]{1,0:T(8,128)S(1)}, f32[8,128]{1,0:T(8,128)S(1)}, bf16[32,128,128]{2,1,0:T(8,128)(2,1)}) custom-call(s32[1]{0:T(128)} %bitcast.x_ref, bf16[32,128,128]{2,1,0:T(8,128)(2,1)S(1)} %copy-done, f32[1,128]{1,0:T(1,128)S(1)} %bitcast.28, ...), custom_call_target="tpu_custom_call", output_to_operand_aliasing={{4}: (16, {})} | custom-call | tf_op jit(solution)/shard_map/backward_blocks/pallas_call | solution.py:345
  33.1 0.0 collective-permute-done.1.rest_0_
  33.1 5.2 %backward_blocks.6 = (f32[128,1024]{1,0:T(8,128)S(1)}, f32[64,512]{1,0:T(8,128)S(1)}, f32[64,128]{1,0:T(8,128)S(1)}, f32[8,128]{1,0:T(8,128)S(1)}, bf16[32,128,128]{2,1,0:T(8,128)(2,1)}) custom-call(s32[1]{0:T(128)} %bitcast.x_ref, bf16[32,128,128]{2,1,0:T(8,128)(2,1)S(1)} %copy-done, f32[1,128]{1,0:T(1,128)S(1)} %bitcast.29, ...), custom_call_target="tpu_custom_call", output_to_operand_aliasing={{4}: (16, {})} | custom-call | tf_op jit(solution)/shard_map/backward_blocks/pallas_call | solution.py:345
  38.3 0.0 collective-permute-done.rest_0_
  38.3 5.4 %backward_blocks.7 = (bf16[1408,128]{1,0:T(8,128)(2,1)S(1)}, bf16[32,128,128]{2,1,0:T(8,128)(2,1)}) custom-call(s32[1]{0:T(128)} %bitcast.x_ref, bf16[32,128,128]{2,1,0:T(8,128)(2,1)S(1)} %copy-done, f32[1,128]{1,0:T(1,128)S(1)} %bitcast.30, f32[1,128]{1,0:T(1,128)S(1)} %bitcast.38, ...), custom_call_target="tpu_custom_call", output_to_operand_aliasing={{1}: (16, {})} | custom-call | tf_op jit(solution)/shard_map/backward_blocks/pallas_call | solution.py:345
  43.7 36.8 %all_to_all.10 = bf16[16,88,128]{2,1,0:T(8,128)(2,1)S(1)} all-to-all(bf16[16,88,128]{2,1,0:T(8,128)(2,1)S(1)} %bitcast.22), channel_id=1, replica_groups=mesh['crop'=8,'z_lo'=4,'x'=4,'z_hi'=4] {'z_lo','x'}, dimensions={0} | all-to-all | bytes 720896 | tf_op jit(solution)/shard_map/all_to_all | solution.py:380
  80.5 0.1 reduce_sum.24
  80.6 19.7 %all-gather = bf16[352,128]{1,0:T(8,128)(2,1)S(1)} all-gather(bf16[88,128]{1,0:T(8,128)(2,1)S(1)} %reduce_sum.24), channel_id=2, replica_groups=mesh['crop'=8,'z_lo'=4,'x'=4,'z_hi'=4] {'z_hi'}, dimensions={0}, use_global_device_ids=true | all-gather | bytes 112640 | tf_op jit(solution)/shard_map/all_gather | solution.py:382
  100.4 14.7 %all_to_all.11 = bf16[16,88,128]{2,1,0:T(8,128)(2,1)S(1)} all-to-all(bf16[16,88,128]{2,1,0:T(8,128)(2,1)S(1)} %broadcast_in_dim.19), channel_id=1, replica_groups=mesh['crop'=8,'z_lo'=4,'x'=4,'z_hi'=4] {'z_lo','x'}, dimensions={0} | all-to-all | bytes 720896 | tf_op jit(solution)/shard_map/all_to_all | solution.py:384
  115.1 1.0 unpack_sums.1
  (2 shorter events, 0.1 us)
Async XLA Ops:
  0.6 5.3 %copy-start = (bf16[32,128,128]{2,1,0:T(8,128)(2,1)S(1)}, bf16[32,128,128]{2,1,0:T(8,128)(2,1)}, u32[]{:S(2)}) copy-start(bf16[32,128,128]{2,1,0:T(8,128)(2,1)} %pair_ref.15) | copy-start | bytes 3145732
  0.7 5.3 %copy-start.1 = (bf16[128,512]{1,0:T(8,128)(2,1)S(1)}, bf16[128,512]{1,0:T(8,128)(2,1)}, u32[]{:S(2)}) copy-start(bf16[128,512]{1,0:T(8,128)(2,1)} %w_gate_ref.15) | copy-start | bytes 393220
  0.7 5.3 %copy-start.2 = (bf16[128,512]{1,0:T(8,128)(2,1)S(1)}, bf16[128,512]{1,0:T(8,128)(2,1)}, u32[]{:S(2)}) copy-start(bf16[128,512]{1,0:T(8,128)(2,1)} %w_up_ref.15) | copy-start | bytes 393220
  0.7 5.3 %copy-start.3 = (bf16[512,128]{1,0:T(8,128)(2,1)S(1)}, bf16[512,128]{1,0:T(8,128)(2,1)}, u32[]{:S(2)}) copy-start(bf16[512,128]{1,0:T(8,128)(2,1)} %w_down_ref.15) | copy-start | bytes 393220
  0.7 5.3 %copy-start.4 = (bf16[128,64]{0,1:T(8,128)(2,1)S(1)}, bf16[128,64]{0,1:T(8,128)(2,1)}, u32[]{:S(2)}) copy-start(bf16[128,64]{0,1:T(8,128)(2,1)} %param.16) | copy-start | bytes 49156
  0.7 5.3 %copy-start.5 = (s32[32,128]{1,0:T(8,128)S(1)}, s32[32,128]{1,0:T(8,128)}, u32[]{:S(2)}) copy-start(s32[32,128]{1,0:T(8,128)} %targets_ref.15) | copy-start | bytes 49156
  0.7 5.3 %copy-start.6 = (s32[32,128]{1,0:T(8,128)S(1)}, s32[32,128]{1,0:T(8,128)}, u32[]{:S(2)}) copy-start(s32[32,128]{1,0:T(8,128)} %mask_ref.15) | copy-start | bytes 49156
  0.7 5.3 %copy-start.7 = (f32[128]{0:T(128)S(1)}, f32[128]{0:T(128)}, u32[]{:S(2)}) copy-start(f32[128]{0:T(128)} %param.11) | copy-start | bytes 1540
  0.7 5.3 %copy-start.8 = (f32[128]{0:T(128)S(1)}, f32[128]{0:T(128)}, u32[]{:S(2)}) copy-start(f32[128]{0:T(128)} %param.12) | copy-start | bytes 1540
  0.7 5.3 %copy-start.9 = (f32[64]{0:T(128)S(1)}, f32[64]{0:T(128)}, u32[]{:S(2)}) copy-start(f32[64]{0:T(128)} %param.17) | copy-start | bytes 772
  4.4 18.7 %collective-permute-start.3 = (bf16[528,128]{1,0:T(8,128)(2,1)}, bf16[528,128]{1,0:T(8,128)(2,1)S(1)}, u32[]{:S(2)}, u32[]{:S(2)}) collective-permute-start(bf16[528,128]{1,0:T(8,128)(2,1)} %forward_send.4), channel_id=1, source_target_pairs={{0,0},{1,16},{2,32},{3,48},{4,4},{5,20},{6,36},{7,52},{8,8},{9,24}... | collective-permute-start | bytes 405512 | tf_op jit(solution)/shard_map/ppermute | solution.py:326
  7.9 20.1 %collective-permute-start.2 = (bf16[528,128]{1,0:T(8,128)(2,1)S(1)}, bf16[528,128]{1,0:T(8,128)(2,1)S(1)}, u32[]{:S(2)}, u32[]{:S(2)}) collective-permute-start(bf16[528,128]{1,0:T(8,128)(2,1)S(1)} %forward_send.5), channel_id=1, source_target_pairs={{0,4},{1,20},{2,36},{3,52},{4,8},{5,24},{6,40},{7,56},{8,12},{9,28... | collective-permute-start | bytes 405512 | tf_op jit(solution)/shard_map/ppermute | solution.py:326
  13.1 20.0 %collective-permute-start.1 = (bf16[528,128]{1,0:T(8,128)(2,1)S(1)}, bf16[528,128]{1,0:T(8,128)(2,1)S(1)}, u32[]{:S(2)}, u32[]{:S(2)}) collective-permute-start(bf16[528,128]{1,0:T(8,128)(2,1)S(1)} %forward_send.6), channel_id=1, source_target_pairs={{0,8},{1,24},{2,40},{3,56},{4,12},{5,28},{6,44},{7,60},{8,0},{9,16... | collective-permute-start | bytes 405512 | tf_op jit(solution)/shard_map/ppermute | solution.py:326
  19.6 18.7 %collective-permute-start = (bf16[528,128]{1,0:T(8,128)(2,1)S(1)}, bf16[528,128]{1,0:T(8,128)(2,1)S(1)}, u32[]{:S(2)}, u32[]{:S(2)}) collective-permute-start(bf16[528,128]{1,0:T(8,128)(2,1)S(1)} %forward_send.7), channel_id=1, source_target_pairs={{0,12},{1,28},{2,44},{3,60},{4,0},{5,16},{6,32},{7,48},{8,4},{9,20... | collective-permute-start | bytes 405512 | tf_op jit(solution)/shard_map/ppermute | solution.py:326
